TPU v7x, 128 devices: a whole 4x4x4 slice. The times are simulated.
128 devices in a mesh: gx: 32 (over z, x, core), yz: 4 (over y).
Axes of the slice: x: 4, y: 4, z: 4, core: 2. Of those that a mesh axis runs over, the one named last changes fastest.
Arguments:
- residuals: float32 [32, 3, 256, 32, 128], P(None, None, 'gx', 'yz'), may hold values from -6 to 6
- vectors: float32 [8, 3, 256, 32, 128], P(None, None, 'gx', 'yz'), may hold values from -0.05 to 1.6
- phases: int32 [256, 32, 128], P('gx', 'yz'), may hold values from 0 to 7
- stiffness: float32 [8], replicated, may hold values from 0.5 to 4
Outputs:
- coarse_coeffs: float32 [1024, 32], P(('gx', 'yz'))
- preconditioned: float32 [32, 3, 256, 32, 128], P(None, None, 'gx', 'yz')
All inputs are finite; a program needn't handle non-finite values.
Results may differ from a plain program's by a relative error of at most 0.0003.
Values sent between devices are 32-bit elements; how exact they have to be, the bound alone decides.
No kernel may reach another device: no remote copies, remote signals or barrier semaphores. Data moves between devices by JAX's collectives and lax.ppermute only.
A program may use at most 192 MiB of HBM per device.

v0:
```python
import functools
import jax
import jax.numpy as jnp
from jax import lax
from jax.experimental import pallas as pl
from jax.experimental.pallas import tpu as pltpu
from jax.sharding import PartitionSpec as P

HIGH = lax.Precision.HIGHEST


def face_weights(modulus_ext):
    centre = modulus_ext[1:-1, 1:-1, :]
    zpadded = jnp.pad(centre, ((0, 0), (0, 0), (1, 1)))
    west_side = 0.5 * (centre + modulus_ext[:-2, 1:-1, :])
    east_side = 0.5 * (centre + modulus_ext[2:, 1:-1, :])
    south_side = 0.5 * (centre + modulus_ext[1:-1, :-2, :])
    north_side = 0.5 * (centre + modulus_ext[1:-1, 2:, :])
    lower_side = 0.5 * (centre + zpadded[:, :, :-2])
    upper_side = 0.5 * (centre + zpadded[:, :, 2:])
    diagonal_sum = 0.002 + west_side + east_side + south_side + north_side + lower_side + upper_side
    return (diagonal_sum, west_side, east_side, south_side, north_side, lower_side, upper_side)


def operate(values, weights):
    diagonal_sum, west_side, east_side, south_side, north_side, lower_side, upper_side = weights
    centre = values[..., 1:-1, 1:-1, :]
    spacing = [(0, 0)] * (values.ndim - 1) + [(1, 1)]
    zpadded = jnp.pad(centre, spacing)
    beside = west_side * values[..., :-2, 1:-1, :] + east_side * values[..., 2:, 1:-1, :]
    beside = beside + south_side * values[..., 1:-1, :-2, :] + north_side * values[..., 1:-1, 2:, :]
    beside = beside + lower_side * zpadded[..., :-2] + upper_side * zpadded[..., 2:]
    return diagonal_sum * centre - beside


def coarse_blocks(vectors_ext, modulus_ext):
    weights = face_weights(modulus_ext[1:-1, 1:-1, :])
    own_cells = vectors_ext[:, :, 2:-2, 2:-2, :]
    isolated = jnp.pad(own_cells, ((0, 0), (0, 0), (1, 1), (1, 1), (0, 0)))
    applied = operate(isolated, weights)
    self_block = jnp.einsum("kcxyz,lcxyz->kl", own_cells, applied, precision=HIGH)
    west_block = -jnp.einsum(
        "kcyz,lcyz->kl",
        weights[1][0] * own_cells[:, :, 0],
        vectors_ext[:, :, 1, 2:-2, :],
        precision=HIGH,
    )
    east_block = -jnp.einsum(
        "kcyz,lcyz->kl",
        weights[2][-1] * own_cells[:, :, -1],
        vectors_ext[:, :, -2, 2:-2, :],
        precision=HIGH,
    )
    south_block = -jnp.einsum(
        "kcxz,lcxz->kl",
        weights[3][:, 0] * own_cells[:, :, :, 0],
        vectors_ext[:, :, 2:-2, 1, :],
        precision=HIGH,
    )
    north_block = -jnp.einsum(
        "kcxz,lcxz->kl",
        weights[4][:, -1] * own_cells[:, :, :, -1],
        vectors_ext[:, :, 2:-2, -2, :],
        precision=HIGH,
    )
    return jnp.stack([self_block, west_block, east_block, south_block, north_block])


def spread(values, column):
    return jnp.broadcast_to(values[:, column : column + 1], values.shape)


def eliminate(work, picks, groups):
    row_index = lax.broadcasted_iota(jnp.int32, (8, 128), 0)

    def turn(step, carry):
        mats = [[work[pick, 8 * i : 8 * i + 8, :] for i in range(groups)] for pick in picks]
        for j in range(0, 8, 2):
            for mat in mats:
                top = mat[0]
                row0 = jnp.broadcast_to(top[j : j + 1, :], (8, 128))
                row1 = jnp.broadcast_to(top[j + 1 : j + 2, :], (8, 128))
                a, b = spread(row0, j), spread(row0, j + 1)
                c, d = spread(row1, j), spread(row1, j + 1)
                inverse = 1.0 / (a * d - b * c)
                new0 = (d * row0 - b * row1) * inverse
                new1 = (a * row1 - c * row0) * inverse
                for i in range(groups):
                    changed = mat[i] - spread(mat[i], j) * new0 - spread(mat[i], j + 1) * new1
                    if i == 0:
                        changed = jnp.where(row_index == j, new0, jnp.where(row_index == j + 1, new1, changed))
                    mat[i] = changed
        for pick, mat in zip(picks, mats):
            for i in range(groups):
                to = (i + groups - 1) % groups
                work[pick, 8 * to : 8 * to + 8, :] = pltpu.roll(mat[i], 120, 1)
        return carry

    lax.fori_loop(0, groups, turn, 0)


def coarse_solve(slabs, size, chunk, rows_ref, out_ref, work, found):
    work[...] = rows_ref[...]
    lane = lax.broadcasted_iota(jnp.int32, (size, 128), 1)
    zeros = jnp.zeros((size, 128), jnp.float32)
    level = 1
    steps = []
    while level < slabs:
        picks = list(range(level, slabs, 2 * level))
        steps.append((level, picks))
        for at in range(0, len(picks), chunk):
            eliminate(work, picks[at : at + chunk], size // 8)
        for keep in range(0, slabs, 2 * level):
            own = work[keep]
            left, right = keep - level, keep + level
            before, after = zeros, zeros
            if left >= 0:
                block = work[left]
                before = jnp.where(
                    lane < size,
                    pltpu.roll(block, 128 - size, 1),
                    jnp.where((lane >= 2 * size) & (lane < 3 * size), 0.0, pltpu.roll(block, size, 1)),
                )
            if right < slabs:
                block = work[right]
                after = jnp.where(
                    lane < size, block, jnp.where(lane < 2 * size, 0.0, pltpu.roll(block, size, 1))
                )
            stack = jnp.concatenate([zeros, before, after, zeros], axis=0)
            change = jnp.dot(own, stack, precision=HIGH, preferred_element_type=jnp.float32)
            kept = jnp.where((lane >= size) & (lane < 3 * size), 0.0, own)
            work[keep] = kept - change
        level *= 2
    eliminate(work, [0], size // 8)
    found[0] = jnp.where(lane < size, pltpu.roll(work[0], 128 - 2 * size, 1), 0.0)
    unit = jnp.where(lane == lax.broadcasted_iota(jnp.int32, (size, 128), 0), 1.0, 0.0)
    for level, picks in reversed(steps):
        for pick in picks:
            left = -found[pick - level]
            right = -found[pick + level] if pick + level < slabs else zeros
            stack = jnp.concatenate([left, right, unit, zeros], axis=0)
            found[pick] = jnp.dot(work[pick], stack, precision=HIGH, preferred_element_type=jnp.float32)
    out_ref[...] = found[:, :, : 128 - 3 * size].reshape(slabs * size, 128 - 3 * size)


def solve_rows(rows, slabs, size, chunk=16):
    shape = (slabs, size, 128)
    return pl.pallas_call(
        functools.partial(coarse_solve, slabs, size, chunk),
        out_shape=jax.ShapeDtypeStruct((slabs * size, 128 - 3 * size), jnp.float32),
        scratch_shapes=[pltpu.VMEM(shape, jnp.float32), pltpu.VMEM(shape, jnp.float32)],
        compiler_params=pltpu.CompilerParams(vmem_limit_bytes=16 * 1024 * 1024),
    )(rows.reshape(shape))


def coarse_rows(blocks, coarse_rhs, spot, count):
    width = blocks.shape[1]
    columns = jnp.arange(count, dtype=jnp.int32)

    def placed(*parts):
        panel = jnp.zeros((width, count, width), jnp.float32)
        for block, offset in parts:
            select = (columns == spot + offset).astype(jnp.float32)
            panel = panel + block[:, None, :] * select[None, :, None]
        return panel.reshape(width, count * width)

    return jnp.concatenate(
        [
            placed((blocks[0], 0), (blocks[3], -1), (blocks[4], 1)),
            placed((blocks[1], 0)),
            placed((blocks[2], 0)),
            coarse_rhs,
        ],
        axis=1,
    )


def sweep_rows(modulus, rows):
    lane = lax.broadcasted_iota(jnp.int32, (10, 128), 1)
    spot = lax.broadcasted_iota(jnp.int32, (10, 128), 0)
    for x in range(10):
        centre = modulus[x + 1, 1:11, :]
        west = 0.5 * (centre + modulus[x, 1:11, :])
        east = 0.5 * (centre + modulus[x + 2, 1:11, :])
        south = 0.5 * (centre + modulus[x + 1, 0:10, :])
        north = 0.5 * (centre + modulus[x + 1, 2:12, :])
        lower = 0.5 * (centre + jnp.where(lane == 0, 0.0, pltpu.roll(centre, 1, 1)))
        upper = 0.5 * (centre + jnp.where(lane == 127, 0.0, pltpu.roll(centre, 127, 1)))
        diagonal = 0.002 + west + east + south + north + lower + upper
        active = centre > 0
        if x in (0, 9):
            active = active & (spot > 0) & (spot < 9)
        scale = jnp.where(active, 0.8 / diagonal, 0.0)
        rows[0, x, 0:10, :] = west * scale
        rows[1, x, 0:10, :] = east * scale
        rows[2, x, 0:10, :] = south * scale
        rows[3, x, 0:10, :] = north * scale
        rows[4, x, 0:10, :] = jnp.where(lane == 0, 0.0, lower * scale)
        rows[5, x, 0:10, :] = jnp.where(lane == 127, 0.0, upper * scale)
        rows[6, x, 0:10, :] = scale


def local_stage(
    place, found, res, vec, own_mod, west, east, south, north, out, modulus, rows, coeff, first, second, scaled
):
    modulus[2:10, 2:10, :] = own_mod[...]
    modulus[0:2, 2:10, :] = west[384:400, :].reshape(2, 8, 128)
    modulus[10:12, 2:10, :] = east[384:400, :].reshape(2, 8, 128)
    for x in range(12):
        modulus[x, 0:2, :] = south[576 + 2 * x : 578 + 2 * x, :]
        modulus[x, 10:12, :] = north[576 + 2 * x : 578 + 2 * x, :]
    sweep_rows(modulus, rows)

    parts = []
    for step_x in range(3):
        for step_y in range(3):
            start = pl.multiple_of(place[step_x * 3 + step_y], 8)
            parts.append(found[pl.ds(start, 8), :])
    near = jnp.concatenate(parts, axis=0)
    near = jnp.concatenate([near, jnp.zeros((72, 96), jnp.float32)], axis=1)
    near = jnp.concatenate([near, jnp.zeros((56, 128), jnp.float32)], axis=0)
    turned = near.T[:32]
    for index in range(72):
        coeff[index] = jnp.broadcast_to(turned[:, index : index + 1], (32, 128))

    def correct(near_index, cell, source, row_of, frozen):
        for comp in range(3):
            total = None
            for k in range(8):
                term = coeff[near_index * 8 + k] * source[pl.ds(row_of(k, comp), 1), :]
                total = term if total is None else total + term
            first[cell, comp * 32 : comp * 32 + 32, :] = total
            if frozen:
                second[cell, comp * 32 : comp * 32 + 32, :] = total

    def own_cell(index, carry):
        x, y = index // 8, index % 8
        correct(4, (x + 2) * 12 + y + 2, vec, lambda k, c: (k * 3 + c) * 64 + index, False)
        return carry

    lax.fori_loop(0, 64, own_cell, 0)

    def edge_cells(y, carry):
        for layer in range(2):
            correct(1, layer * 12 + y + 2, west, lambda k, c: ((k * 3 + c) * 2 + layer) * 8 + y, layer == 0)
            correct(7, (10 + layer) * 12 + y + 2, east, lambda k, c: ((k * 3 + c) * 2 + layer) * 8 + y, layer == 1)
            correct(3, (y + 2) * 12 + layer, south, lambda k, c: ((k * 3 + c) * 12 + y + 2) * 2 + layer, layer == 0)
            correct(5, (y + 2) * 12 + 10 + layer, north, lambda k, c: ((k * 3 + c) * 12 + y + 2) * 2 + layer, layer == 1)
        return carry

    lax.fori_loop(0, 8, edge_cells, 0)
    for x, near_x in ((1, 0), (10, 6)):
        correct(near_x, x * 12 + 1, south, lambda k, c: ((k * 3 + c) * 12 + x) * 2 + 1, True)
        correct(near_x + 2, x * 12 + 10, north, lambda k, c: ((k * 3 + c) * 12 + x) * 2, True)

    def scale_cell(x, y, source, start, stride):
        weight = rows[6, x, pl.ds(y, 1), :]
        for comp in range(3):
            scaled[x * 10 + y, comp * 32 : comp * 32 + 32, :] = (
                source[pl.ds(start(comp), 32, stride=stride), :] * weight
            )

    def own_scaled(index, carry):
        x, y = index // 8, index % 8
        scale_cell(x + 1, y + 1, res, lambda c: c * 64 + index, 192)
        return carry

    lax.fori_loop(0, 64, own_scaled, 0)

    def edge_scaled(y, carry):
        scale_cell(0, y + 1, west, lambda c: 400 + c * 8 + y, 24)
        scale_cell(9, y + 1, east, lambda c: 400 + c * 8 + y, 24)
        scale_cell(y + 1, 0, south, lambda c: 600 + c * 8 + y, 24)
        scale_cell(y + 1, 9, north, lambda c: 600 + c * 8 + y, 24)
        return carry

    lax.fori_loop(0, 8, edge_scaled, 0)

    def relax(x, y, source, store):
        cell = (x + 1) * 12 + y + 1
        weight = [rows[i, x, pl.ds(y, 1), :] for i in range(6)]
        for comp in range(3):
            span = slice(comp * 32, comp * 32 + 32)
            here = source[cell, span, :]
            value = 0.2 * here + scaled[x * 10 + y, span, :]
            value = value + weight[0] * source[cell - 12, span, :] + weight[1] * source[cell + 12, span, :]
            value = value + weight[2] * source[cell - 1, span, :] + weight[3] * source[cell + 1, span, :]
            value = value + weight[4] * pltpu.roll(here, 1, 1) + weight[5] * pltpu.roll(here, 127, 1)
            store(comp, span, value)

    for source, target in ((first, second), (second, first), (first, second)):

        def sweep(x, y, source=source, target=target):
            def keep(comp, span, value):
                target[(x + 1) * 12 + y + 1, span, :] = value

            relax(x, y, source, keep)

        def inner(index, carry, sweep=sweep):
            sweep(index // 10 + 1, index % 10)
            return carry

        def outer(y, carry, sweep=sweep):
            sweep(0, y)
            sweep(9, y)
            return carry

        lax.fori_loop(0, 80, inner, 0)
        lax.fori_loop(1, 9, outer, 0)

    def last(index, carry):
        def keep(comp, span, value):
            out[pl.ds(comp * 64 + index, 32, stride=192), :] = value

        relax(index // 8 + 1, index % 8 + 1, second, keep)
        return carry

    lax.fori_loop(0, 64, last, 0)


def local_parts(place, found, residuals, vectors, modulus, west, east, south, north):
    whole = pl.BlockSpec(memory_space=pltpu.VMEM)
    result = pl.pallas_call(
        local_stage,
        out_shape=jax.ShapeDtypeStruct((6144, 128), jnp.float32),
        in_specs=[pl.BlockSpec(memory_space=pltpu.SMEM)] + [whole] * 8,
        out_specs=whole,
        scratch_shapes=[
            pltpu.VMEM((12, 16, 128), jnp.float32),
            pltpu.VMEM((7, 10, 16, 128), jnp.float32),
            pltpu.VMEM((72, 32, 128), jnp.float32),
            pltpu.VMEM((144, 96, 128), jnp.float32),
            pltpu.VMEM((144, 96, 128), jnp.float32),
            pltpu.VMEM((100, 96, 128), jnp.float32),
        ],
        compiler_params=pltpu.CompilerParams(vmem_limit_bytes=48 * 1024 * 1024),
    )(
        place,
        found,
        residuals.reshape(6144, 128),
        vectors.reshape(1536, 128),
        modulus,
        west,
        east,
        south,
        north,
    )
    return result.reshape(residuals.shape)


def shifted(values, axis, step):
    count = lax.axis_size(axis)
    return lax.ppermute(values, axis, [(i, i + step) for i in range(count) if 0 <= i + step < count])


def lines(*arrays):
    return jnp.concatenate([array.reshape(-1, 128) for array in arrays], axis=0)


def on_device(residuals, vectors, phases, stiffness):
    count_x = lax.axis_size("gx")
    count_y = lax.axis_size("yz")
    count = count_x * count_y
    index_x = lax.axis_index("gx")
    index_y = lax.axis_index("yz")
    width = vectors.shape[0]
    levels = stiffness.shape[0]
    choose = (phases[None] == jnp.arange(levels, dtype=jnp.int32)[:, None, None, None]).astype(
        jnp.float32
    )
    modulus = jnp.sum(stiffness[:, None, None, None] * choose, axis=0)
    west = shifted(lines(vectors[:, :, 6:8], modulus[6:8], residuals[:, :, 7]), "gx", 1)
    east = shifted(lines(vectors[:, :, 0:2], modulus[0:2], residuals[:, :, 0]), "gx", -1)
    wide_vectors = jnp.concatenate(
        [west[:384].reshape(8, 3, 2, 8, 128), vectors, east[:384].reshape(8, 3, 2, 8, 128)], axis=2
    )
    wide_modulus = jnp.concatenate(
        [west[384:400].reshape(2, 8, 128), modulus, east[384:400].reshape(2, 8, 128)], axis=0
    )
    south = shifted(lines(wide_vectors[:, :, :, 6:8], wide_modulus[:, 6:8], residuals[:, :, :, 7]), "yz", 1)
    north = shifted(lines(wide_vectors[:, :, :, 0:2], wide_modulus[:, 0:2], residuals[:, :, :, 0]), "yz", -1)
    vectors_ext = jnp.concatenate(
        [south[:576].reshape(8, 3, 12, 2, 128), wide_vectors, north[:576].reshape(8, 3, 12, 2, 128)], axis=3
    )
    modulus_ext = jnp.concatenate(
        [south[576:600].reshape(12, 2, 128), wide_modulus, north[576:600].reshape(12, 2, 128)], axis=1
    )
    blocks = coarse_blocks(vectors_ext, modulus_ext)
    coarse_rhs = jnp.einsum("kcxyz,rcxyz->kr", vectors, residuals, precision=HIGH)
    own_rows = coarse_rows(blocks, coarse_rhs, index_y, count_y)
    every = jnp.broadcast_to(own_rows[None], (count,) + own_rows.shape)
    rows = lax.all_to_all(every, ("gx", "yz"), 0, 0)
    coeffs_all = solve_rows(rows, count_x, count_y * width)
    coeffs = lax.dynamic_slice_in_dim(coeffs_all, (index_x * count_y + index_y) * width, width, 0)
    near_x = jnp.clip(index_x + jnp.arange(-1, 2), 0, count_x - 1)
    near_y = jnp.clip(index_y + jnp.arange(-1, 2), 0, count_y - 1)
    place = ((near_x[:, None] * count_y + near_y[None, :]) * width).reshape(9).astype(jnp.int32)
    result = local_parts(place, coeffs_all, residuals, vectors, modulus, west, east, south, north)
    return (coeffs, result)


def solution(mesh):
    return jax.shard_map(
        on_device,
        mesh=mesh,
        in_specs=(
            P(None, None, "gx", "yz", None),
            P(None, None, "gx", "yz", None),
            P("gx", "yz", None),
            P(),
        ),
        out_specs=(P(("gx", "yz"), None), P(None, None, "gx", "yz", None)),
        check_vma=False,
    )
```

profile of v0, /device:TPU:1, one launch (start us, length us, event | category | flops | bytes accessed | tf_op | source)
XLA Modules:
  0.0 147.6 jit_solution(326065407182465819)
XLA Ops:
  0.6 0.9 select_reduce_fusion.own_mod
  1.5 1.2 fusion.47
  2.7 1.1 fusion.48
  3.9 3.3 %collective-permute-start.1 = (f32[1168,128]{1,0:T(8,128)S(1)}, f32[1168,128]{1,0:T(8,128)S(1)}, u32[]{:S(2)}, u32[]{:S(2)}) collective-permute-start(f32[1168,128]{1,0:T(8,128)S(1)} %pad_maximum_fusion.3), channel_id=1, source_target_pairs={{4,0},{8,4},{12,8},{16,12},{20,16},{24,20},{28,24},{32,28},{36,32}... | collective-permute-start | bytes 1794056 | tf_op jit(solution)/shard_map/ppermute | solution.py:353
  7.3 3.1 %collective-permute-start = (f32[1168,128]{1,0:T(8,128)S(1)}, f32[1168,128]{1,0:T(8,128)S(1)}, u32[]{:S(2)}, u32[]{:S(2)}) collective-permute-start(f32[1168,128]{1,0:T(8,128)S(1)} %pad_maximum_fusion.2), channel_id=1, source_target_pairs={{0,4},{4,8},{8,12},{12,16},{16,20},{20,24},{24,28},{28,32},{32,36}... | collective-permute-start | bytes 1794056 | tf_op jit(solution)/shard_map/ppermute | solution.py:353
  10.4 3.7 %fusion.46 = (f32[32,3,8,1,128]{4,3,2,1,0:T(1,128)S(1)}, f32[32,3,8,1,128]{4,3,2,1,0:T(1,128)S(1)}) fusion(f32[32,3,8,8,128]{4,3,2,1,0:T(8,128)} %param.4), kind=kLoop, calls=%fused_computation.98 | loop fusion | bytes 1572864 | tf_op jit(solution)/shard_map/slice | solution.py:381
  14.1 2.0 %collective-permute-done.1.east = f32[1168,128]{1,0:T(8,128)S(1)} collective-permute-done((f32[1168,128]{1,0:T(8,128)S(1)}, f32[1168,128]{1,0:T(8,128)S(1)}, u32[]{:S(2)}, u32[]{:S(2)}) %collective-permute-start.1) | collective-permute-done | bytes 598048 | tf_op jit(solution)/shard_map/ppermute | solution.py:353
  16.1 1.2 collective-permute-done.west
  17.4 0.2 pad_maximum_fusion.4
  17.5 0.6 copy-done.1
  18.1 0.9 pad_maximum_fusion
  19.0 3.2 %collective-permute-start.2 = (f32[1368,128]{1,0:T(8,128)}, f32[1368,128]{1,0:T(8,128)S(1)}, u32[]{:S(2)}, u32[]{:S(2)}) collective-permute-start(f32[1368,128]{1,0:T(8,128)} %pad_maximum_fusion), channel_id=1, source_target_pairs={{0,1},{1,2},{2,3},{4,5},{5,6},{6,7},{8,9},{9,10},{10,11},{12,13},{... | collective-permute-start | bytes 2101256 | tf_op jit(solution)/shard_map/ppermute | solution.py:353
  22.3 0.9 pad_maximum_fusion.1
  23.2 1.3 collective-permute-start.3
  25.0 6.1 %fusion.2 = f32[8,32]{1,0:T(8,128)S(1)} fusion(f32[32,3,8,8,128]{4,3,2,1,0:T(8,128)} %param.4, f32[8,3,8,8,128]{4,3,2,1,0:T(8,128)S(1)} %copy-done), kind=kOutput, calls=%fused_computation.9 | convolution fusion | flops 75497472 | bytes 3933184 | tf_op jit(solution)/shard_map/kcxyz,rcxyz->kr/dot_general | solution.py:389
  31.1 3.6 %collective-permute-done.2.south = f32[1368,128]{1,0:T(8,128)S(1)} collective-permute-done((f32[1368,128]{1,0:T(8,128)}, f32[1368,128]{1,0:T(8,128)S(1)}, u32[]{:S(2)}, u32[]{:S(2)}) %collective-permute-start.2) | collective-permute-done | bytes 700448 | tf_op jit(solution)/shard_map/ppermute | solution.py:353
  34.8 4.9 %collective-permute-done.3.north = f32[1368,128]{1,0:T(8,128)S(1)} collective-permute-done((f32[1368,128]{1,0:T(8,128)}, f32[1368,128]{1,0:T(8,128)S(1)}, u32[]{:S(2)}, u32[]{:S(2)}) %collective-permute-start.3) | collective-permute-done | bytes 700448 | tf_op jit(solution)/shard_map/ppermute | solution.py:353
  39.8 0.3 fusion.5
  40.1 0.1 mul.303
  40.2 0.3 fusion.6
  40.7 0.5 fusion.12
  41.2 2.3 %convolution_bitcast_fusion = f32[8,8]{0,1:T(8,128)S(1)} fusion(f32[8,3,8,8,128]{4,3,2,1,0:T(8,128)S(1)} %fusion.12, f32[8,3,8,8,128]{4,3,2,1,0:T(8,128)S(1)} %copy-done), kind=kOutput, calls=%fused_computation.8 | convolution fusion | flops 18874368 | bytes 1573120 | tf_op jit(solution)/shard_map/kcxyz,lcxyz->kl/dot_general | solution.py:41
  43.9 0.3 fusion.8
  44.2 0.1 mul.276
  44.4 0.3 fusion.7
  44.9 0.8 broadcast_in_dim.2
  45.8 15.0 %all-to-all-start = ((f32[128,8,128]{2,1,0:T(8,128)}), f32[128,8,128]{2,1,0:T(8,128)S(1)}, u32[]{:S(2)}, u32[]{:S(2)}) async-start(f32[128,8,128]{2,1,0:T(8,128)} %broadcast_in_dim.2), calls=%async_computation | async-start | bytes 1048576 | tf_op jit(solution)/shard_map/all_to_all | solution.py:392
  61.0 13.6 %all-to-all-done = f32[128,8,128]{2,1,0:T(8,128)S(1)} async-done(((f32[128,8,128]{2,1,0:T(8,128)}), f32[128,8,128]{2,1,0:T(8,128)S(1)}, u32[]{:S(2)}, u32[]{:S(2)}) %all-to-all-start) | async-done | bytes 524320 | tf_op jit(solution)/shard_map/all_to_all | solution.py:392
  74.5 22.7 %shard_map.59.found = f32[1024,32]{1,0:T(8,128)S(1)} custom-call(f32[32,32,128]{2,1,0:T(8,128)S(1)} %bitcast.87), custom_call_target="tpu_custom_call" | custom-call | tf_op jit(solution)/shard_map/pallas_call | solution.py:148
  97.3 0.6 constant_dynamic-slice_fusion
  97.9 1.1 copy-done.2
  98.9 48.7 %shard_map.60 = f32[6144,128]{1,0:T(8,128)} custom-call(s32[9]{0:T(128)S(1)} %mul.309.place, f32[1024,32]{1,0:T(8,128)S(1)} %shard_map.59.found, f32[6144,128]{1,0:T(8,128)} %bitcast.88, f32[1536,128]{1,0:T(8,128)S(1)} %bitcast.86, f32[8,8,128]{2,1,0:T(8,128)S(1)} %select_reduce_fusion.own_mod, f32[1168,128]{1,0:T(8,128)S(1)} %copy-done.2, ...), custom_call_target="tpu_custom_call" | custom-call | tf_op jit(solution)/shard_map/pallas_call | solution.py:323
  (49 shorter events, 1.9 us)
Async XLA Ops:
  2.7 14.6 %copy-start = (f32[8,3,8,8,128]{4,3,2,1,0:T(8,128)S(1)}, f32[8,3,8,8,128]{4,3,2,1,0:T(8,128)}, u32[]{:S(2)}) copy-start(f32[8,3,8,8,128]{4,3,2,1,0:T(8,128)} %param.5) | copy-start | bytes 2359300
  3.9 12.2 %collective-permute-start.1 = (f32[1168,128]{1,0:T(8,128)S(1)}, f32[1168,128]{1,0:T(8,128)S(1)}, u32[]{:S(2)}, u32[]{:S(2)}) collective-permute-start(f32[1168,128]{1,0:T(8,128)S(1)} %pad_maximum_fusion.3), channel_id=1, source_target_pairs={{4,0},{8,4},{12,8},{16,12},{20,16},{24,20},{28,24},{32,28},{36,32}... | collective-permute-start | bytes 1794056 | tf_op jit(solution)/shard_map/ppermute | solution.py:353
  7.3 10.0 %collective-permute-start = (f32[1168,128]{1,0:T(8,128)S(1)}, f32[1168,128]{1,0:T(8,128)S(1)}, u32[]{:S(2)}, u32[]{:S(2)}) collective-permute-start(f32[1168,128]{1,0:T(8,128)S(1)} %pad_maximum_fusion.2), channel_id=1, source_target_pairs={{0,4},{4,8},{8,12},{12,16},{16,20},{20,24},{24,28},{28,32},{32,36}... | collective-permute-start | bytes 1794056 | tf_op jit(solution)/shard_map/ppermute | solution.py:353
  17.3 0.8 copy-start.1
  19.0 15.7 %collective-permute-start.2 = (f32[1368,128]{1,0:T(8,128)}, f32[1368,128]{1,0:T(8,128)S(1)}, u32[]{:S(2)}, u32[]{:S(2)}) collective-permute-start(f32[1368,128]{1,0:T(8,128)} %pad_maximum_fusion), channel_id=1, source_target_pairs={{0,1},{1,2},{2,3},{4,5},{5,6},{6,7},{8,9},{9,10},{10,11},{12,13},{... | collective-permute-start | bytes 2101256 | tf_op jit(solution)/shard_map/ppermute | solution.py:353
  23.2 16.5 %collective-permute-start.3 = (f32[1368,128]{1,0:T(8,128)}, f32[1368,128]{1,0:T(8,128)S(1)}, u32[]{:S(2)}, u32[]{:S(2)}) collective-permute-start(f32[1368,128]{1,0:T(8,128)} %pad_maximum_fusion.1), channel_id=1, source_target_pairs={{1,0},{2,1},{3,2},{5,4},{6,5},{7,6},{9,8},{10,9},{11,10},{13,12},{... | collective-permute-start | bytes 2101256 | tf_op jit(solution)/shard_map/ppermute | solution.py:353
  45.8 28.8 %all-to-all-start = ((f32[128,8,128]{2,1,0:T(8,128)}), f32[128,8,128]{2,1,0:T(8,128)S(1)}, u32[]{:S(2)}, u32[]{:S(2)}) async-start(f32[128,8,128]{2,1,0:T(8,128)} %broadcast_in_dim.2), calls=%async_computation | async-start | bytes 1048576 | tf_op jit(solution)/shard_map/all_to_all | solution.py:392
  97.9 1.1 copy-start.2
where the time goes:
time: 148 us
  Pallas kernels  71.4 us (48%)
  starting transfers between devices  25.9 us (18%)
  waiting for transfers between devices  25.3 us (17%)
  local copies, waits for them, and re-layouts  10.7 us (7%)
  matrix products  9.45 us (6%)
  other arithmetic  3.89 us (3%)
    pallas_call x1, Pallas kernels, local_parts(): pl.pallas_call(local_stage, out_shape=jax.ShapeDtypeStruct((6144, 128), j...  48.7 us
    pallas_call x1, Pallas kernels, solve_rows(): pl.pallas_call(functools.partial(coarse_solve, slabs, size, chunk), out_s...  22.7 us
    all_to_all x1, starting transfers between devices, on_device(): rows = lax.all_to_all(every, ('gx', 'yz'), 0, 0)  15 us
    all_to_all x1, waiting for transfers between devices, on_device(): rows = lax.all_to_all(every, ('gx', 'yz'), 0, 0)  13.6 us
    ppermute x4, waiting for transfers between devices, shifted(): lax.ppermute(values, axis, [(i, i + step) for i in range(count) if 0 <= i...  11.8 us
    ppermute x4, starting transfers between devices, shifted(): lax.ppermute(values, axis, [(i, i + step) for i in range(count) if 0 <= i...  10.9 us
    dot_general x1, matrix products, on_device(): jnp.einsum('kcxyz,rcxyz->kr', vectors, residuals, precision=HIGH)  6.13 us
    slice x1, local copies, waits for them, and re-layouts, on_device(): residuals[:, :, :, 0]  3.68 us
  transfers between devices with their start and end apart: 5, of which 5 were waited for; matrix products, arithmetic and copies ran while one was open for 8% of the time, Pallas kernels for 0%

commit v1 on v0

--- a/solution.py
+++ b/solution.py
@@ -7,88 +7,50 @@
 from jax.sharding import PartitionSpec as P
 
 HIGH = lax.Precision.HIGHEST
-
-
-def face_weights(modulus_ext):
-    centre = modulus_ext[1:-1, 1:-1, :]
-    zpadded = jnp.pad(centre, ((0, 0), (0, 0), (1, 1)))
-    west_side = 0.5 * (centre + modulus_ext[:-2, 1:-1, :])
-    east_side = 0.5 * (centre + modulus_ext[2:, 1:-1, :])
-    south_side = 0.5 * (centre + modulus_ext[1:-1, :-2, :])
-    north_side = 0.5 * (centre + modulus_ext[1:-1, 2:, :])
-    lower_side = 0.5 * (centre + zpadded[:, :, :-2])
-    upper_side = 0.5 * (centre + zpadded[:, :, 2:])
-    diagonal_sum = 0.002 + west_side + east_side + south_side + north_side + lower_side + upper_side
-    return (diagonal_sum, west_side, east_side, south_side, north_side, lower_side, upper_side)
-
-
-def operate(values, weights):
-    diagonal_sum, west_side, east_side, south_side, north_side, lower_side, upper_side = weights
-    centre = values[..., 1:-1, 1:-1, :]
-    spacing = [(0, 0)] * (values.ndim - 1) + [(1, 1)]
-    zpadded = jnp.pad(centre, spacing)
-    beside = west_side * values[..., :-2, 1:-1, :] + east_side * values[..., 2:, 1:-1, :]
-    beside = beside + south_side * values[..., 1:-1, :-2, :] + north_side * values[..., 1:-1, 2:, :]
-    beside = beside + lower_side * zpadded[..., :-2] + upper_side * zpadded[..., 2:]
-    return diagonal_sum * centre - beside
-
-
-def coarse_blocks(vectors_ext, modulus_ext):
-    weights = face_weights(modulus_ext[1:-1, 1:-1, :])
-    own_cells = vectors_ext[:, :, 2:-2, 2:-2, :]
-    isolated = jnp.pad(own_cells, ((0, 0), (0, 0), (1, 1), (1, 1), (0, 0)))
-    applied = operate(isolated, weights)
-    self_block = jnp.einsum("kcxyz,lcxyz->kl", own_cells, applied, precision=HIGH)
-    west_block = -jnp.einsum(
-        "kcyz,lcyz->kl",
-        weights[1][0] * own_cells[:, :, 0],
-        vectors_ext[:, :, 1, 2:-2, :],
-        precision=HIGH,
-    )
-    east_block = -jnp.einsum(
-        "kcyz,lcyz->kl",
-        weights[2][-1] * own_cells[:, :, -1],
-        vectors_ext[:, :, -2, 2:-2, :],
-        precision=HIGH,
-    )
-    south_block = -jnp.einsum(
-        "kcxz,lcxz->kl",
-        weights[3][:, 0] * own_cells[:, :, :, 0],
-        vectors_ext[:, :, 2:-2, 1, :],
-        precision=HIGH,
-    )
-    north_block = -jnp.einsum(
-        "kcxz,lcxz->kl",
-        weights[4][:, -1] * own_cells[:, :, :, -1],
-        vectors_ext[:, :, 2:-2, -2, :],
-        precision=HIGH,
-    )
-    return jnp.stack([self_block, west_block, east_block, south_block, north_block])
+GROUP = 5
 
 
 def spread(values, column):
     return jnp.broadcast_to(values[:, column : column + 1], values.shape)
 
 
+def fill(values, row):
+    return jnp.broadcast_to(values[row : row + 1, :], values.shape)
+
+
 def eliminate(work, picks, groups):
     row_index = lax.broadcasted_iota(jnp.int32, (8, 128), 0)
 
     def turn(step, carry):
         mats = [[work[pick, 8 * i : 8 * i + 8, :] for i in range(groups)] for pick in picks]
-        for j in range(0, 8, 2):
+        for j in (0, 4):
             for mat in mats:
-                top = mat[0]
-                row0 = jnp.broadcast_to(top[j : j + 1, :], (8, 128))
-                row1 = jnp.broadcast_to(top[j + 1 : j + 2, :], (8, 128))
-                a, b = spread(row0, j), spread(row0, j + 1)
-                c, d = spread(row1, j), spread(row1, j + 1)
-                inverse = 1.0 / (a * d - b * c)
-                new0 = (d * row0 - b * row1) * inverse
-                new1 = (a * row1 - c * row0) * inverse
+                cols = [[spread(mat[i], j + q) for q in range(4)] for i in range(groups)]
+                r0, r1, r2, r3 = [fill(mat[0], j + q) for q in range(4)]
+                p = [[fill(cols[0][q], j + i) for q in range(i + 1)] for i in range(4)]
+                inverse = 1.0 / (p[0][0] * p[1][1] - p[1][0] * p[1][0])
+                a0, a1, a2 = p[1][1] * inverse, -p[1][0] * inverse, p[0][0] * inverse
+                y00 = p[2][0] * a0 + p[2][1] * a1
+                y01 = p[2][0] * a1 + p[2][1] * a2
+                y10 = p[3][0] * a0 + p[3][1] * a1
+                y11 = p[3][0] * a1 + p[3][1] * a2
+                s0 = p[2][2] - (y00 * p[2][0] + y01 * p[2][1])
+                s1 = p[3][2] - (y10 * p[2][0] + y11 * p[2][1])
+                s2 = p[3][3] - (y10 * p[3][0] + y11 * p[3][1])
+                inverse = 1.0 / (s0 * s2 - s1 * s1)
+                t2 = r2 - (y00 * r0 + y01 * r1)
+                t3 = r3 - (y10 * r0 + y11 * r1)
+                n2 = (s2 * t2 - s1 * t3) * inverse
+                n3 = (s0 * t3 - s1 * t2) * inverse
+                u0 = r0 - (p[2][0] * n2 + p[3][0] * n3)
+                u1 = r1 - (p[2][1] * n2 + p[3][1] * n3)
+                n0 = a0 * u0 + a1 * u1
+                n1 = a1 * u0 + a2 * u1
                 for i in range(groups):
-                    changed = mat[i] - spread(mat[i], j) * new0 - spread(mat[i], j + 1) * new1
+                    changed = mat[i] - ((cols[i][0] * n0 + cols[i][1] * n1) + (cols[i][2] * n2 + cols[i][3] * n3))
                     if i == 0:
-                        changed = jnp.where(row_index == j, new0, jnp.where(row_index == j + 1, new1, changed))
+                        for q, new in enumerate((n0, n1, n2, n3)):
+                            changed = jnp.where(row_index == j + q, new, changed)
                     mat[i] = changed
         for pick, mat in zip(picks, mats):
             for i in range(groups):
@@ -99,8 +61,41 @@
     lax.fori_loop(0, groups, turn, 0)
 
 
+def assemble(slabs, groups, rows_ref, work):
+    lane = lax.broadcasted_iota(jnp.int32, (8, 128), 1)
+
+    def within(start, width):
+        return (lane >= start) & (lane < start + width)
+
+    def slab(g, first):
+        for h in range(groups):
+            block = rows_ref[g * groups + h]
+            mine = within(8 * h, min(16, 32 - 8 * h)) | within(64 + 8 * h, 8) | (lane >= 96)
+            total = jnp.where(mine, block, 0.0)
+            if h > 0:
+                below = rows_ref[g * groups + h - 1]
+                moved = pltpu.roll(below, 56, 1)
+                extra = moved if h < 3 else pltpu.roll(below, 88, 1)
+                total = total + jnp.where(within(8 * h - 8, 8), moved, jnp.where(within(8 * h, 8), extra, 0.0))
+            if not first:
+                before = rows_ref[(g - 1) * groups + h]
+                moved = pltpu.roll(before, 88 if h < 3 else 120, 1)
+                total = total + jnp.where(
+                    within(8 * h, 8), moved, jnp.where(within(32 + 8 * h, 8), before, 0.0)
+                )
+            work[g, 8 * h : 8 * h + 8, :] = total
+
+    slab(0, True)
+
+    def later(g, carry):
+        slab(g, False)
+        return carry
+
+    lax.fori_loop(1, slabs, later, 0)
+
+
 def coarse_solve(slabs, size, chunk, rows_ref, out_ref, work, found):
-    work[...] = rows_ref[...]
+    assemble(slabs, size // 8, rows_ref, work)
     lane = lax.broadcasted_iota(jnp.int32, (size, 128), 1)
     zeros = jnp.zeros((size, 128), jnp.float32)
     level = 1
@@ -150,29 +145,148 @@
         out_shape=jax.ShapeDtypeStruct((slabs * size, 128 - 3 * size), jnp.float32),
         scratch_shapes=[pltpu.VMEM(shape, jnp.float32), pltpu.VMEM(shape, jnp.float32)],
         compiler_params=pltpu.CompilerParams(vmem_limit_bytes=16 * 1024 * 1024),
-    )(rows.reshape(shape))
-
-
-def coarse_rows(blocks, coarse_rhs, spot, count):
-    width = blocks.shape[1]
-    columns = jnp.arange(count, dtype=jnp.int32)
-
-    def placed(*parts):
-        panel = jnp.zeros((width, count, width), jnp.float32)
-        for block, offset in parts:
-            select = (columns == spot + offset).astype(jnp.float32)
-            panel = panel + block[:, None, :] * select[None, :, None]
-        return panel.reshape(width, count * width)
-
-    return jnp.concatenate(
-        [
-            placed((blocks[0], 0), (blocks[3], -1), (blocks[4], 1)),
-            placed((blocks[1], 0)),
-            placed((blocks[2], 0)),
-            coarse_rhs,
-        ],
-        axis=1,
+        cost_estimate=pl.CostEstimate(flops=20_000_000_000, bytes_accessed=90_000_000, transcendentals=0),
+    )(rows)
+
+
+def lane_sums(stack):
+    ones = jnp.ones((8, 128), jnp.float32)
+    return lax.dot_general(
+        ones, stack, (((1,), (1,)), ((), ())), precision=HIGH, preferred_element_type=jnp.float32
     )
+
+
+def panel_of(parts):
+    row = lax.broadcasted_iota(jnp.int32, (8, 128), 0)
+    panel = jnp.zeros((8, 128), jnp.float32)
+    for k in range(8):
+        panel = jnp.where(row == k, lane_sums(jnp.concatenate(parts(k), axis=0)), panel)
+    return panel
+
+
+def project(vec, res, out):
+    def cell(index, totals):
+        block = res[pl.ds(index, 32, stride=192), :]
+        return tuple(totals[k] + block * vec[pl.ds(k * 192 + index, 1), :] for k in range(8))
+
+    totals = lax.fori_loop(0, 192, cell, tuple(jnp.zeros((32, 128), jnp.float32) for _ in range(8)))
+    blank = jnp.zeros((96, 128), jnp.float32)
+    out[...] = panel_of(lambda k: [blank, totals[k]])
+
+
+def coarse_panel(spot, vec, modulus, east, north, known, out, rows, turned):
+    lane = lax.broadcasted_iota(jnp.int32, (8, 128), 1)
+    place = lax.broadcasted_iota(jnp.int32, (8, 128), 0)
+    for x in range(8):
+        centre = modulus[x]
+        half = 0.5 * centre
+        west = 0.5 * (centre + modulus[x - 1]) if x > 0 else half
+        east_row = modulus[x + 1] if x < 7 else east[192:200, :]
+        east_side = 0.5 * (centre + east_row)
+        south = 0.5 * (centre + jnp.where(place == 0, 0.0, pltpu.roll(centre, 1, 0)))
+        beyond = jnp.broadcast_to(north[192 + x : 193 + x, :], (8, 128))
+        north_side = 0.5 * (centre + jnp.where(place == 7, beyond, pltpu.roll(centre, 7, 0)))
+        lower = 0.5 * (centre + jnp.where(lane == 0, 0.0, pltpu.roll(centre, 1, 1)))
+        upper = 0.5 * (centre + jnp.where(lane == 127, 0.0, pltpu.roll(centre, 127, 1)))
+        span = slice(8 * x, 8 * x + 8)
+        rows[0, span, :] = west if x > 0 else jnp.zeros((8, 128), jnp.float32)
+        rows[1, span, :] = east_side if x < 7 else jnp.zeros((8, 128), jnp.float32)
+        rows[2, span, :] = jnp.where(place == 0, 0.0, south)
+        rows[3, span, :] = jnp.where(place == 7, 0.0, north_side)
+        rows[4, span, :] = jnp.where(lane == 0, 0.0, lower)
+        rows[5, span, :] = jnp.where(lane == 127, 0.0, upper)
+        rows[6, span, :] = 0.002 + west + east_side + south + north_side + lower + upper
+        rows[7, span, :] = east_side
+        rows[8, span, :] = north_side
+
+    def gather(index, carry):
+        turned[index] = vec[pl.ds(index, 8, stride=192), :]
+        return carry
+
+    lax.fori_loop(0, 192, gather, 0, unroll=4)
+
+    def own(index):
+        return turned[index]
+
+    zero = jnp.zeros((8, 128), jnp.float32)
+
+    def cell(index, totals):
+        at = index % 64
+        weight = [rows[i, pl.ds(at, 1), :] for i in range(7)]
+        here = own(index)
+        applied = weight[6] * here - weight[4] * pltpu.roll(here, 1, 1) - weight[5] * pltpu.roll(here, 127, 1)
+        applied = applied - weight[0] * own(jnp.maximum(index - 8, 0))
+        applied = applied - weight[1] * own(jnp.minimum(index + 8, 191))
+        applied = applied - weight[2] * own(jnp.maximum(index - 1, 0))
+        applied = applied - weight[3] * own(jnp.minimum(index + 1, 191))
+        return tuple(totals[k] + applied * vec[pl.ds(k * 192 + index, 1), :] for k in range(8))
+
+    inside = lax.fori_loop(0, 192, cell, (zero,) * 8, unroll=2)
+
+    def face(source, first, step, side):
+        def spot_of(index, totals):
+            comp, at = index // 8, index % 8
+            cell_row = first + at * step
+            mine = comp * 64 + cell_row
+            weight = rows[side, pl.ds(cell_row, 1), :]
+            half = 0.5 * modulus[cell_row // 8, pl.ds(cell_row % 8, 1), :]
+            here = own(mine)
+            there = source[pl.ds(index, 8, stride=24), :]
+            toward, back, extra = -weight * there, -weight * here, half * there
+            new = []
+            for k in range(8):
+                here_k = vec[pl.ds(k * 192 + mine, 1), :]
+                there_k = source[pl.ds(k * 24 + index, 1), :]
+                new += [
+                    totals[3 * k] + toward * here_k,
+                    totals[3 * k + 1] + back * there_k,
+                    totals[3 * k + 2] + extra * there_k,
+                ]
+            return tuple(new)
+
+        return lax.fori_loop(0, 24, spot_of, (zero,) * 24)
+
+    easts = face(east, 56, 1, 7)
+    norths = face(north, 7, 8, 8)
+
+    def parts(k):
+        return [
+            inside[k], norths[3 * k], zero, zero,
+            easts[3 * k + 1], easts[3 * k + 2], zero, zero,
+            easts[3 * k], norths[3 * k + 1], norths[3 * k + 2], zero,
+            zero, zero, zero, zero,
+        ]
+
+    panel = panel_of(parts)
+    placed = panel
+    for h in range(1, 4):
+        ahead = pltpu.roll(panel, 8 * h, 1)
+        behind = pltpu.roll(panel, 128 + 8 * h - 32, 1)
+        moved = jnp.where(lane % 32 >= 8 * h, ahead, behind)
+        placed = jnp.where(spot[0] == h, moved, placed)
+    out[...] = jnp.broadcast_to((placed + known[...])[None], out.shape)
+
+
+def coarse_rows(spot, residuals, vectors, modulus, east, north, count):
+    whole = pl.BlockSpec(memory_space=pltpu.VMEM)
+    vec = vectors.reshape(1536, 128)
+    known = pl.pallas_call(
+        project,
+        out_shape=jax.ShapeDtypeStruct((8, 128), jnp.float32),
+        in_specs=[whole, whole],
+        out_specs=whole,
+        compiler_params=pltpu.CompilerParams(vmem_limit_bytes=16 * 1024 * 1024),
+        cost_estimate=pl.CostEstimate(flops=12_600_000, bytes_accessed=4_000_000, transcendentals=0),
+    )(vec, residuals.reshape(6144, 128))
+    return pl.pallas_call(
+        coarse_panel,
+        out_shape=jax.ShapeDtypeStruct((count, 8, 128), jnp.float32),
+        in_specs=[pl.BlockSpec(memory_space=pltpu.SMEM)] + [whole] * 5,
+        out_specs=whole,
+        scratch_shapes=[pltpu.VMEM((9, 64, 128), jnp.float32), pltpu.VMEM((192, 8, 128), jnp.float32)],
+        compiler_params=pltpu.CompilerParams(vmem_limit_bytes=16 * 1024 * 1024),
+        cost_estimate=pl.CostEstimate(flops=6_000_000, bytes_accessed=2_000_000, transcendentals=0),
+    )(spot, vec, modulus, east, north, known)
 
 
 def sweep_rows(modulus, rows):
@@ -201,7 +315,7 @@
 
 
 def local_stage(
-    place, found, res, vec, own_mod, west, east, south, north, out, modulus, rows, coeff, first, second, scaled
+    place, found, res, vec, own_mod, west, east, south, north, out, modulus, rows, coeff, first, second, scaled, shift
 ):
     modulus[2:10, 2:10, :] = own_mod[...]
     modulus[0:2, 2:10, :] = west[384:400, :].reshape(2, 8, 128)
@@ -276,46 +390,57 @@
 
     lax.fori_loop(0, 8, edge_scaled, 0)
 
-    def relax(x, y, source, store):
+    up = lax.broadcasted_iota(jnp.int32, (256, 256), 0) % 128
+    to = lax.broadcasted_iota(jnp.int32, (256, 256), 1)
+    moves = ((to < 128) & (to == up + 1)) | ((to >= 128) & (to - 128 == up - 1))
+    shift[...] = jnp.where(moves, 1.0, 0.0).astype(jnp.bfloat16)
+
+    def relax(x, y, cells, source, store):
         cell = (x + 1) * 12 + y + 1
-        weight = [rows[i, x, pl.ds(y, 1), :] for i in range(6)]
-        for comp in range(3):
-            span = slice(comp * 32, comp * 32 + 32)
-            here = source[cell, span, :]
-            value = 0.2 * here + scaled[x * 10 + y, span, :]
-            value = value + weight[0] * source[cell - 12, span, :] + weight[1] * source[cell + 12, span, :]
-            value = value + weight[2] * source[cell - 1, span, :] + weight[3] * source[cell + 1, span, :]
-            value = value + weight[4] * pltpu.roll(here, 1, 1) + weight[5] * pltpu.roll(here, 127, 1)
-            store(comp, span, value)
+        block = source[pl.ds(cell, cells)].reshape(cells * 96, 128)
+        high = block.astype(jnp.bfloat16)
+        rest = (block - high.astype(jnp.float32)).astype(jnp.bfloat16)
+        moved = jnp.dot(
+            jnp.concatenate([high, rest], axis=1), shift[...], preferred_element_type=jnp.float32
+        )
+        for n in range(cells):
+            weight = [rows[i, x, pl.ds(y + n, 1), :] for i in range(6)]
+            here = moved[n * 96 : n * 96 + 96]
+            value = 0.2 * source[cell + n] + scaled[x * 10 + y + n]
+            value = value + weight[0] * source[cell + n - 12] + weight[1] * source[cell + n + 12]
+            value = value + weight[2] * source[cell + n - 1] + weight[3] * source[cell + n + 1]
+            value = value + weight[4] * here[:, :128] + weight[5] * here[:, 128:]
+            store(n, value)
 
     for source, target in ((first, second), (second, first), (first, second)):
 
-        def sweep(x, y, source=source, target=target):
-            def keep(comp, span, value):
-                target[(x + 1) * 12 + y + 1, span, :] = value
-
-            relax(x, y, source, keep)
+        def sweep(x, y, cells, source=source, target=target):
+            def keep(n, value):
+                target[(x + 1) * 12 + y + n + 1] = value
+
+            relax(x, y, cells, source, keep)
 
         def inner(index, carry, sweep=sweep):
-            sweep(index // 10 + 1, index % 10)
+            for y in range(0, 10, GROUP):
+                sweep(index + 1, y, GROUP)
             return carry
 
-        def outer(y, carry, sweep=sweep):
-            sweep(0, y)
-            sweep(9, y)
-            return carry
-
-        lax.fori_loop(0, 80, inner, 0)
-        lax.fori_loop(1, 9, outer, 0)
-
-    def last(index, carry):
-        def keep(comp, span, value):
-            out[pl.ds(comp * 64 + index, 32, stride=192), :] = value
-
-        relax(index // 8 + 1, index % 8 + 1, second, keep)
-        return carry
-
-    lax.fori_loop(0, 64, last, 0)
+        lax.fori_loop(0, 8, inner, 0)
+        for x in (0, 9):
+            for y in range(1, 9, 4):
+                sweep(x, y, 4)
+
+    def last(x, carry):
+        for y in range(0, 8, 4):
+
+            def keep(n, value, y=y):
+                for comp in range(3):
+                    out[pl.ds(comp * 64 + x * 8 + y + n, 32, stride=192), :] = value[comp * 32 : comp * 32 + 32]
+
+            relax(x + 1, y + 1, 4, second, keep)
+        return carry
+
+    lax.fori_loop(0, 8, last, 0)
 
 
 def local_parts(place, found, residuals, vectors, modulus, west, east, south, north):
@@ -332,6 +457,7 @@
             pltpu.VMEM((144, 96, 128), jnp.float32),
             pltpu.VMEM((144, 96, 128), jnp.float32),
             pltpu.VMEM((100, 96, 128), jnp.float32),
+            pltpu.VMEM((256, 256), jnp.bfloat16),
         ],
         compiler_params=pltpu.CompilerParams(vmem_limit_bytes=48 * 1024 * 1024),
     )(
@@ -347,7 +473,6 @@
     )
     return result.reshape(residuals.shape)
 
-
 def shifted(values, axis, step):
     count = lax.axis_size(axis)
     return lax.ppermute(values, axis, [(i, i + step) for i in range(count) if 0 <= i + step < count])
@@ -369,8 +494,16 @@
         jnp.float32
     )
     modulus = jnp.sum(stiffness[:, None, None, None] * choose, axis=0)
-    west = shifted(lines(vectors[:, :, 6:8], modulus[6:8], residuals[:, :, 7]), "gx", 1)
-    east = shifted(lines(vectors[:, :, 0:2], modulus[0:2], residuals[:, :, 0]), "gx", -1)
+    east_face = shifted(lines(vectors[:, :, 0], modulus[0]), "gx", -1)
+    north_face = shifted(lines(vectors[:, :, :, 0], modulus[:, 0]), "yz", -1)
+    spot = index_y.astype(jnp.int32).reshape(1)
+    every = coarse_rows(spot, residuals, vectors, modulus, east_face, north_face, count)
+    to_west = lines(vectors[:, :, 0:2], modulus[0:2], residuals[:, :, 0])
+    to_east = lines(vectors[:, :, 6:8], modulus[6:8], residuals[:, :, 7])
+    every, to_west, to_east = lax.optimization_barrier((every, to_west, to_east))
+    rows = lax.all_to_all(every, ("gx", "yz"), 0, 0)
+    west = shifted(to_east, "gx", 1)
+    east = shifted(to_west, "gx", -1)
     wide_vectors = jnp.concatenate(
         [west[:384].reshape(8, 3, 2, 8, 128), vectors, east[:384].reshape(8, 3, 2, 8, 128)], axis=2
     )
@@ -379,17 +512,6 @@
     )
     south = shifted(lines(wide_vectors[:, :, :, 6:8], wide_modulus[:, 6:8], residuals[:, :, :, 7]), "yz", 1)
     north = shifted(lines(wide_vectors[:, :, :, 0:2], wide_modulus[:, 0:2], residuals[:, :, :, 0]), "yz", -1)
-    vectors_ext = jnp.concatenate(
-        [south[:576].reshape(8, 3, 12, 2, 128), wide_vectors, north[:576].reshape(8, 3, 12, 2, 128)], axis=3
-    )
-    modulus_ext = jnp.concatenate(
-        [south[576:600].reshape(12, 2, 128), wide_modulus, north[576:600].reshape(12, 2, 128)], axis=1
-    )
-    blocks = coarse_blocks(vectors_ext, modulus_ext)
-    coarse_rhs = jnp.einsum("kcxyz,rcxyz->kr", vectors, residuals, precision=HIGH)
-    own_rows = coarse_rows(blocks, coarse_rhs, index_y, count_y)
-    every = jnp.broadcast_to(own_rows[None], (count,) + own_rows.shape)
-    rows = lax.all_to_all(every, ("gx", "yz"), 0, 0)
     coeffs_all = solve_rows(rows, count_x, count_y * width)
     coeffs = lax.dynamic_slice_in_dim(coeffs_all, (index_x * count_y + index_y) * width, width, 0)
     near_x = jnp.clip(index_x + jnp.arange(-1, 2), 0, count_x - 1)

time: 148 us -> 120 us (0.81)
  waiting for transfers between devices: 25.3 us -> 1.41 us
  matrix products: 9.45 us -> 0 us
  Pallas kernels: 71.4 us -> 68.5 us
  local copies, waits for them, and re-layouts: 10.7 us -> 13.5 us
  starting transfers between devices: 25.9 us -> 28.7 us
  other arithmetic: 3.89 us -> 6.28 us
    pallas_call x1, Pallas kernels: 48.7 us -> 27.1 us  [local_parts(): pl.pallas_call(local_stage, out_shape=jax.ShapeDtypeStruct((6144, 128), j...]
    pallas_call x0 -> x2, Pallas kernels: none -> 18.6 us  [the longest x1 10.9 us: coarse_rows(): pl.pallas_call(coarse_panel, out_shape=jax.ShapeDtypeStruct((count, 8, 12...]
    all_to_all x1, waiting for transfers between devices: 13.6 us -> 1.39 us  [on_device(): rows = lax.all_to_all(every, ('gx', 'yz'), 0, 0)]
    ppermute x4 -> x6, waiting for transfers between devices: 11.8 us -> 0.02 us  [shifted(): lax.ppermute(values, axis, [(i, i + step) for i in range(count) if 0 <= i...]
    dot_general x6 -> x0, matrix products: 9.45 us -> none  [the longest x1 6.13 us: on_device(): jnp.einsum('kcxyz,rcxyz->kr', vectors, residuals, precision=HIGH)]
    ppermute x4 -> x6, starting transfers between devices: 10.9 us -> 15.4 us  [shifted(): lax.ppermute(values, axis, [(i, i + step) for i in range(count) if 0 <= i...]
    slice x1, local copies, waits for them, and re-layouts: 3.68 us -> 1.4 us  [on_device(): residuals[:, :, :, 0]]
    unnamed x6 -> x16, local copies, waits for them, and re-layouts: 1.65 us -> 3.8 us
  transfers between devices with their start and end apart: 5 -> 7, of which waited for: 5 -> 1; matrix products, arithmetic and copies ran while one was open for 8% -> 12% of each run, Pallas kernels for 0% -> 26%
where the time goes in v1:
time: 120 us; the launch traced here: 119 us
  Pallas kernels  68.5 us (57%)
  starting transfers between devices  28.7 us (24%)
  local copies, waits for them, and re-layouts  13.5 us (11%)
  other arithmetic  6.28 us (5%)
  waiting for transfers between devices  1.41 us (1%)
    pallas_call x1, Pallas kernels, local_parts(): pl.pallas_call(local_stage, out_shape=jax.ShapeDtypeStruct((6144, 128), j...  27.1 us
    pallas_call x1, Pallas kernels, solve_rows(): pl.pallas_call(functools.partial(coarse_solve, slabs, size, chunk), out_s...  22.8 us
    ppermute x6, starting transfers between devices, shifted(): lax.ppermute(values, axis, [(i, i + step) for i in range(count) if 0 <= i...  15.4 us
    all_to_all x1, starting transfers between devices, on_device(): rows = lax.all_to_all(every, ('gx', 'yz'), 0, 0)  13.4 us
    pallas_call x1, Pallas kernels, coarse_rows(): pl.pallas_call(coarse_panel, out_shape=jax.ShapeDtypeStruct((count, 8, 12...  10.9 us
    pallas_call x1, Pallas kernels, coarse_rows(): pl.pallas_call(project, out_shape=jax.ShapeDtypeStruct((8, 128), jnp.floa...  7.66 us
    unnamed x16, local copies, waits for them, and re-layouts  3.8 us
    concatenate x5, other arithmetic, lines(): return jnp.concatenate([array.reshape(-1, 128) for array in arrays], axis=0)  3.59 us
  transfers between devices with their start and end apart: 7, of which 1 were waited for; matrix products, arithmetic and copies ran while one was open for 12% of the time, Pallas kernels for 26%

profile of v1, /device:TPU:1, one launch (start us, length us, event | category | flops | bytes accessed | tf_op | source)
XLA Modules:
  0.0 119.3 jit_solution(1975977221022394902)
XLA Ops:
  0.6 1.0 select_reduce_fusion.modulus.own_mod
  1.7 0.9 slice.60
  2.6 3.3 %collective-permute-start = (f32[200,128]{1,0:T(8,128)S(1)}, f32[200,128]{1,0:T(8,128)S(1)}, u32[]{:S(2)}, u32[]{:S(2)}) collective-permute-start(f32[200,128]{1,0:T(8,128)S(1)} %pad_maximum_fusion.7), channel_id=1, source_target_pairs={{4,0},{8,4},{12,8},{16,12},{20,16},{24,20},{28,24},{32,28},{36,32}... | collective-permute-start | bytes 307208 | tf_op jit(solution)/shard_map/ppermute | solution.py:478
  5.9 1.2 slice.62
  7.1 0.7 pad_maximum_fusion.8
  7.8 1.3 %collective-permute-start.1 = (f32[200,128]{1,0:T(8,128)}, f32[200,128]{1,0:T(8,128)S(1)}, u32[]{:S(2)}, u32[]{:S(2)}) collective-permute-start(f32[200,128]{1,0:T(8,128)} %pad_maximum_fusion.8), channel_id=1, source_target_pairs={{1,0},{2,1},{3,2},{5,4},{6,5},{7,6},{9,8},{10,9},{11,10},{13,12},{... | collective-permute-start | bytes 307208 | tf_op jit(solution)/shard_map/ppermute | solution.py:478
  9.1 1.1 fusion.2
  10.2 1.2 fusion.1
  11.3 1.1 pad_maximum_fusion.2
  12.4 1.1 copy-done.1
  13.6 7.7 %shard_map.59.known = f32[8,128]{1,0:T(8,128)S(1)} custom-call(f32[1536,128]{1,0:T(8,128)S(1)} %bitcast.33, f32[6144,128]{1,0:T(8,128)S(1)} %bitcast.32), custom_call_target="tpu_custom_call" | custom-call | flops 12600000 | bytes 4000000 | tf_op jit(solution)/shard_map/pallas_call | solution.py:273
  21.2 10.9 %shard_map.60 = f32[128,8,128]{2,1,0:T(8,128)S(1)} custom-call(s32[1]{0:T(128)} %bitcast.spot, f32[1536,128]{1,0:T(8,128)S(1)} %bitcast.34, f32[8,8,128]{2,1,0:T(8,128)S(1)} %select_reduce_fusion.modulus.own_mod, f32[200,128]{1,0:T(8,128)S(1)} %collective-permute-done.east, f32[200,128]{1,0:T(8,128)S(1)} %collective-permute-done.1.north, ...), custom_call_target="tpu_custom_call" | custom-call | flops 6000000 | bytes 2000000 | tf_op jit(solution)/shard_map/pallas_call | solution.py:281
  32.2 0.8 copy-done.3
  33.0 3.1 %collective-permute-start.2 = (f32[1168,128]{1,0:T(8,128)}, f32[1168,128]{1,0:T(8,128)}, u32[]{:S(2)}, u32[]{:S(2)}) collective-permute-start(f32[1168,128]{1,0:T(8,128)} %get-tuple-element.6), channel_id=1, source_target_pairs={{0,4},{4,8},{8,12},{12,16},{16,20},{20,24},{24,28},{28,32},{32,36}... | collective-permute-start | bytes 1794056 | tf_op jit(solution)/shard_map/ppermute | solution.py:478
  36.1 2.0 %collective-permute-start.3 = (f32[1168,128]{1,0:T(8,128)}, f32[1168,128]{1,0:T(8,128)}, u32[]{:S(2)}, u32[]{:S(2)}) collective-permute-start(f32[1168,128]{1,0:T(8,128)} %get-tuple-element.7), channel_id=1, source_target_pairs={{4,0},{8,4},{12,8},{16,12},{20,16},{24,20},{28,24},{32,28},{36,32}... | collective-permute-start | bytes 1794056 | tf_op jit(solution)/shard_map/ppermute | solution.py:478
  38.3 1.4 %fusion = (f32[32,3,8,1,128]{4,3,2,1,0:T(1,128)}, f32[32,3,8,1,128]{4,3,2,1,0:T(1,128)}) fusion(f32[32,3,8,8,128]{4,3,2,1,0:T(8,128)S(1)} %copy-done), kind=kLoop, calls=%fused_computation.24 | loop fusion | bytes 1572864 | tf_op jit(solution)/shard_map/slice | solution.py:514
  39.7 13.4 %all-to-all-start = ((f32[128,8,128]{2,1,0:T(8,128)}), f32[128,8,128]{2,1,0:T(8,128)S(1)}, u32[]{:S(2)}, u32[]{:S(2)}) async-start(f32[128,8,128]{2,1,0:T(8,128)} %copy-done.3), calls=%async_computation | async-start | bytes 1048576 | tf_op jit(solution)/shard_map/all_to_all | solution.py:504
  53.1 0.9 slice.84
  54.0 0.9 slice.85
  55.0 1.6 %pad_maximum_fusion.4 = (f32[8,3,12,2,128]{4,3,2,1,0:T(2,128)S(1)}, f32[8,3,12,2,128]{4,3,2,1,0:T(2,128)S(1)}) fusion(f32[8,3,2,8,128]{4,3,2,1,0:T(8,128)S(1)} %bitcast.44, f32[8,3,8,8,128]{4,3,2,1,0:T(8,128)} %param.5, f32[8,3,2,8,128]{4,3,2,1,0:T(8,128)S(1)} %bitcast.43), kind=kLoop, calls=%fused_computation.4 | loop fusion | flops 294912 | bytes 1769472 | tf_op jit(solution)/shard_map/concatenate | solution.py:507
  56.6 0.7 slice_bitcast_fusion
  57.3 0.7 slice_bitcast_fusion.1
  58.0 0.9 pad_maximum_fusion.1
  58.9 1.3 %collective-permute-start.5 = (f32[1368,128]{1,0:T(8,128)}, f32[1368,128]{1,0:T(8,128)S(1)}, u32[]{:S(2)}, u32[]{:S(2)}) collective-permute-start(f32[1368,128]{1,0:T(8,128)} %pad_maximum_fusion.1), channel_id=1, source_target_pairs={{1,0},{2,1},{3,2},{5,4},{6,5},{7,6},{9,8},{10,9},{11,10},{13,12},{... | collective-permute-start | bytes 2101256 | tf_op jit(solution)/shard_map/ppermute | solution.py:478
  60.2 0.9 pad_maximum_fusion
  61.1 4.3 %collective-permute-start.4 = (f32[1368,128]{1,0:T(8,128)}, f32[1368,128]{1,0:T(8,128)S(1)}, u32[]{:S(2)}, u32[]{:S(2)}) collective-permute-start(f32[1368,128]{1,0:T(8,128)} %pad_maximum_fusion), channel_id=1, source_target_pairs={{0,1},{1,2},{2,3},{4,5},{5,6},{6,7},{8,9},{9,10},{10,11},{12,13},{... | collective-permute-start | bytes 2101256 | tf_op jit(solution)/shard_map/ppermute | solution.py:478
  65.4 1.4 %all-to-all-done.rows_ref = f32[128,8,128]{2,1,0:T(8,128)S(1)} async-done(((f32[128,8,128]{2,1,0:T(8,128)}), f32[128,8,128]{2,1,0:T(8,128)S(1)}, u32[]{:S(2)}, u32[]{:S(2)}) %all-to-all-start) | async-done | bytes 524320 | tf_op jit(solution)/shard_map/all_to_all | solution.py:504
  66.8 0.8 copy-done.4
  67.6 1.0 copy-done.5
  68.7 22.8 %shard_map.61.found = f32[1024,32]{1,0:T(8,128)S(1)} custom-call(f32[128,8,128]{2,1,0:T(8,128)S(1)} %copy-done.5), custom_call_target="tpu_custom_call" | custom-call | flops 20000000000 | bytes 90000000 | tf_op jit(solution)/shard_map/pallas_call | solution.py:143
  91.5 0.6 constant_dynamic-slice_fusion
  92.1 27.1 %shard_map.62 = f32[6144,128]{1,0:T(8,128)} custom-call(s32[9]{0:T(128)S(1)} %mul.35.place, f32[1024,32]{1,0:T(8,128)S(1)} %shard_map.61.found, f32[6144,128]{1,0:T(8,128)} %bitcast.31, f32[1536,128]{1,0:T(8,128)S(1)} %bitcast.35, f32[8,8,128]{2,1,0:T(8,128)S(1)} %select_reduce_fusion.modulus.own_mod, f32[1168,128]{1,0:T(8,128)} %collective-permute-done.2.west, ...), custom_call_target="tpu_custom_call" | custom-call | tf_op jit(solution)/shard_map/pallas_call | solution.py:448
  (26 shorter events, 0.2 us)
Async XLA Ops:
  0.6 11.8 %copy-start = (f32[32,3,8,8,128]{4,3,2,1,0:T(8,128)S(1)}, f32[32,3,8,8,128]{4,3,2,1,0:T(8,128)}, u32[]{:S(2)}) copy-start(f32[32,3,8,8,128]{4,3,2,1,0:T(8,128)} %param.4) | copy-start | bytes 9437188
  2.6 18.6 %collective-permute-start = (f32[200,128]{1,0:T(8,128)S(1)}, f32[200,128]{1,0:T(8,128)S(1)}, u32[]{:S(2)}, u32[]{:S(2)}) collective-permute-start(f32[200,128]{1,0:T(8,128)S(1)} %pad_maximum_fusion.7), channel_id=1, source_target_pairs={{4,0},{8,4},{12,8},{16,12},{20,16},{24,20},{28,24},{32,28},{36,32}... | collective-permute-start | bytes 307208 | tf_op jit(solution)/shard_map/ppermute | solution.py:478
  7.8 13.4 %collective-permute-start.1 = (f32[200,128]{1,0:T(8,128)}, f32[200,128]{1,0:T(8,128)S(1)}, u32[]{:S(2)}, u32[]{:S(2)}) collective-permute-start(f32[200,128]{1,0:T(8,128)} %pad_maximum_fusion.8), channel_id=1, source_target_pairs={{1,0},{2,1},{3,2},{5,4},{6,5},{7,6},{9,8},{10,9},{11,10},{13,12},{... | collective-permute-start | bytes 307208 | tf_op jit(solution)/shard_map/ppermute | solution.py:478
  12.4 1.1 copy-start.1
  32.2 0.8 copy-start.3
  33.0 20.1 %collective-permute-start.2 = (f32[1168,128]{1,0:T(8,128)}, f32[1168,128]{1,0:T(8,128)}, u32[]{:S(2)}, u32[]{:S(2)}) collective-permute-start(f32[1168,128]{1,0:T(8,128)} %get-tuple-element.6), channel_id=1, source_target_pairs={{0,4},{4,8},{8,12},{12,16},{16,20},{20,24},{24,28},{28,32},{32,36}... | collective-permute-start | bytes 1794056 | tf_op jit(solution)/shard_map/ppermute | solution.py:478
  36.1 18.0 %collective-permute-start.3 = (f32[1168,128]{1,0:T(8,128)}, f32[1168,128]{1,0:T(8,128)}, u32[]{:S(2)}, u32[]{:S(2)}) collective-permute-start(f32[1168,128]{1,0:T(8,128)} %get-tuple-element.7), channel_id=1, source_target_pairs={{4,0},{8,4},{12,8},{16,12},{20,16},{24,20},{28,24},{32,28},{36,32}... | collective-permute-start | bytes 1794056 | tf_op jit(solution)/shard_map/ppermute | solution.py:478
  39.7 18.3 %copy-start.7 = (f32[32,3,8,1,128]{4,3,2,1,0:T(1,128)S(1)}, f32[32,3,8,1,128]{4,3,2,1,0:T(1,128)}, u32[]{:S(2)}) copy-start(f32[32,3,8,1,128]{4,3,2,1,0:T(1,128)} %get-tuple-element.8) | copy-start | bytes 1179652
  39.7 20.5 %copy-start.6 = (f32[32,3,8,1,128]{4,3,2,1,0:T(1,128)S(1)}, f32[32,3,8,1,128]{4,3,2,1,0:T(1,128)}, u32[]{:S(2)}) copy-start(f32[32,3,8,1,128]{4,3,2,1,0:T(1,128)} %get-tuple-element.9) | copy-start | bytes 1179652
  39.7 27.1 %all-to-all-start = ((f32[128,8,128]{2,1,0:T(8,128)}), f32[128,8,128]{2,1,0:T(8,128)S(1)}, u32[]{:S(2)}, u32[]{:S(2)}) async-start(f32[128,8,128]{2,1,0:T(8,128)} %copy-done.3), calls=%async_computation | async-start | bytes 1048576 | tf_op jit(solution)/shard_map/all_to_all | solution.py:504
  58.9 33.2 %collective-permute-start.5 = (f32[1368,128]{1,0:T(8,128)}, f32[1368,128]{1,0:T(8,128)S(1)}, u32[]{:S(2)}, u32[]{:S(2)}) collective-permute-start(f32[1368,128]{1,0:T(8,128)} %pad_maximum_fusion.1), channel_id=1, source_target_pairs={{1,0},{2,1},{3,2},{5,4},{6,5},{7,6},{9,8},{10,9},{11,10},{13,12},{... | collective-permute-start | bytes 2101256 | tf_op jit(solution)/shard_map/ppermute | solution.py:478
  61.1 31.0 %copy-start.2 = (f32[8,3,8,8,128]{4,3,2,1,0:T(8,128)S(1)}, f32[8,3,8,8,128]{4,3,2,1,0:T(8,128)}, u32[]{:S(2)}) copy-start(f32[8,3,8,8,128]{4,3,2,1,0:T(8,128)} %param.5) | copy-start | bytes 2359300
  61.1 31.0 %collective-permute-start.4 = (f32[1368,128]{1,0:T(8,128)}, f32[1368,128]{1,0:T(8,128)S(1)}, u32[]{:S(2)}, u32[]{:S(2)}) collective-permute-start(f32[1368,128]{1,0:T(8,128)} %pad_maximum_fusion), channel_id=1, source_target_pairs={{0,1},{1,2},{2,3},{4,5},{5,6},{6,7},{8,9},{9,10},{10,11},{12,13},{... | collective-permute-start | bytes 2101256 | tf_op jit(solution)/shard_map/ppermute | solution.py:478
  66.8 0.8 copy-start.4
  67.6 1.0 copy-start.5

commit v2 on v1

--- a/solution.py
+++ b/solution.py
@@ -94,7 +94,7 @@
     lax.fori_loop(1, slabs, later, 0)
 
 
-def coarse_solve(slabs, size, chunk, rows_ref, out_ref, work, found):
+def coarse_solve(slabs, size, chunk, spot, rows_ref, own_ref, near_ref, work, found):
     assemble(slabs, size // 8, rows_ref, work)
     lane = lax.broadcasted_iota(jnp.int32, (size, 128), 1)
     zeros = jnp.zeros((size, 128), jnp.float32)
@@ -127,41 +127,66 @@
             work[keep] = kept - change
         level *= 2
     eliminate(work, [0], size // 8)
+    found[...] = jnp.zeros(found.shape, jnp.float32)
     found[0] = jnp.where(lane < size, pltpu.roll(work[0], 128 - 2 * size, 1), 0.0)
     unit = jnp.where(lane == lax.broadcasted_iota(jnp.int32, (size, 128), 0), 1.0, 0.0)
+    lowest = jnp.maximum(spot[0] - 1, 0)
     for level, picks in reversed(steps):
-        for pick in picks:
-            left = -found[pick - level]
-            right = -found[pick + level] if pick + level < slabs else zeros
+        first = lowest // level
+        first = first + 1 - first % 2
+        for wanted in (first, first + 2)[: len(picks)]:
+            pick = jnp.minimum(wanted, slabs // level - 1) * level
+            left, right = -found[pick - level], -found[pick + level]
             stack = jnp.concatenate([left, right, unit, zeros], axis=0)
             found[pick] = jnp.dot(work[pick], stack, precision=HIGH, preferred_element_type=jnp.float32)
-    out_ref[...] = found[:, :, : 128 - 3 * size].reshape(slabs * size, 128 - 3 * size)
-
-
-def solve_rows(rows, slabs, size, chunk=16):
-    shape = (slabs, size, 128)
+    width = 128 - 3 * size
+
+    def taken(slab, row):
+        return found[slab, pl.ds(pl.multiple_of(row * 8, 8), 8), :][:, :width]
+
+    own_ref[...] = taken(spot[0], spot[1])
+    for step_x in range(3):
+        for step_y in range(3):
+            slab = jnp.clip(spot[0] + step_x - 1, 0, slabs - 1)
+            row = jnp.clip(spot[1] + step_y - 1, 0, size // 8 - 1)
+            at = (step_x * 3 + step_y) * 8
+            near_ref[at : at + 8, :] = taken(slab, row)
+
+
+def solve_rows(spot, rows, slabs, size, chunk=16):
+    width = 128 - 3 * size
+    whole = pl.BlockSpec(memory_space=pltpu.VMEM)
     return pl.pallas_call(
         functools.partial(coarse_solve, slabs, size, chunk),
-        out_shape=jax.ShapeDtypeStruct((slabs * size, 128 - 3 * size), jnp.float32),
-        scratch_shapes=[pltpu.VMEM(shape, jnp.float32), pltpu.VMEM(shape, jnp.float32)],
+        out_shape=(
+            jax.ShapeDtypeStruct((8, width), jnp.float32),
+            jax.ShapeDtypeStruct((72, width), jnp.float32),
+        ),
+        in_specs=[pl.BlockSpec(memory_space=pltpu.SMEM), whole],
+        out_specs=(whole, whole),
+        scratch_shapes=[
+            pltpu.VMEM((slabs, size, 128), jnp.float32),
+            pltpu.VMEM((slabs + 1, size, 128), jnp.float32),
+        ],
         compiler_params=pltpu.CompilerParams(vmem_limit_bytes=16 * 1024 * 1024),
         cost_estimate=pl.CostEstimate(flops=20_000_000_000, bytes_accessed=90_000_000, transcendentals=0),
-    )(rows)
-
-
-def lane_sums(stack):
-    ones = jnp.ones((8, 128), jnp.float32)
-    return lax.dot_general(
-        ones, stack, (((1,), (1,)), ((), ())), precision=HIGH, preferred_element_type=jnp.float32
-    )
-
-
-def panel_of(parts):
-    row = lax.broadcasted_iota(jnp.int32, (8, 128), 0)
-    panel = jnp.zeros((8, 128), jnp.float32)
-    for k in range(8):
-        panel = jnp.where(row == k, lane_sums(jnp.concatenate(parts(k), axis=0)), panel)
-    return panel
+    )(spot, rows)
+
+
+def panel_of(slots):
+    lane = lax.broadcasted_iota(jnp.int32, (8, 128), 1)
+    stack = jnp.concatenate([part for parts in slots for part in parts], axis=0)
+    ones = jnp.ones((128, 128), jnp.float32)
+    sums = jnp.dot(stack, ones, precision=HIGH, preferred_element_type=jnp.float32)
+    columns = []
+    at = 0
+    for parts in slots:
+        column = jnp.zeros((8, 128), jnp.float32)
+        for k in range(len(parts)):
+            column = jnp.where(lane == k, sums[at : at + 8], column)
+            at += 8
+        columns.append(column)
+    return jnp.concatenate(columns, axis=0).T[:8]
 
 
 def project(vec, res, out):
@@ -169,9 +194,9 @@
         block = res[pl.ds(index, 32, stride=192), :]
         return tuple(totals[k] + block * vec[pl.ds(k * 192 + index, 1), :] for k in range(8))
 
-    totals = lax.fori_loop(0, 192, cell, tuple(jnp.zeros((32, 128), jnp.float32) for _ in range(8)))
-    blank = jnp.zeros((96, 128), jnp.float32)
-    out[...] = panel_of(lambda k: [blank, totals[k]])
+    totals = lax.fori_loop(0, 192, cell, tuple(jnp.zeros((32, 128), jnp.float32) for _ in range(8)), unroll=4)
+    slots = [[totals[k][8 * i : 8 * i + 8] for k in range(8)] for i in range(4)]
+    out[...] = panel_of([[]] * 12 + slots)
 
 
 def coarse_panel(spot, vec, modulus, east, north, known, out, rows, turned):
@@ -221,7 +246,7 @@
         applied = applied - weight[3] * own(jnp.minimum(index + 1, 191))
         return tuple(totals[k] + applied * vec[pl.ds(k * 192 + index, 1), :] for k in range(8))
 
-    inside = lax.fori_loop(0, 192, cell, (zero,) * 8, unroll=2)
+    inside = lax.fori_loop(0, 192, cell, (zero,) * 8, unroll=8)
 
     def face(source, first, step, side):
         def spot_of(index, totals):
@@ -249,21 +274,20 @@
     easts = face(east, 56, 1, 7)
     norths = face(north, 7, 8, 8)
 
-    def parts(k):
-        return [
-            inside[k], norths[3 * k], zero, zero,
-            easts[3 * k + 1], easts[3 * k + 2], zero, zero,
-            easts[3 * k], norths[3 * k + 1], norths[3 * k + 2], zero,
-            zero, zero, zero, zero,
+    panel = panel_of(
+        [
+            inside, norths[0::3], [], [],
+            easts[1::3], easts[2::3], [], [],
+            easts[0::3], norths[1::3], norths[2::3], [],
+            [], [], [], [],
         ]
-
-    panel = panel_of(parts)
+    )
     placed = panel
     for h in range(1, 4):
         ahead = pltpu.roll(panel, 8 * h, 1)
         behind = pltpu.roll(panel, 128 + 8 * h - 32, 1)
         moved = jnp.where(lane % 32 >= 8 * h, ahead, behind)
-        placed = jnp.where(spot[0] == h, moved, placed)
+        placed = jnp.where(spot[1] == h, moved, placed)
     out[...] = jnp.broadcast_to((placed + known[...])[None], out.shape)
 
 
@@ -315,7 +339,7 @@
 
 
 def local_stage(
-    place, found, res, vec, own_mod, west, east, south, north, out, modulus, rows, coeff, first, second, scaled, shift
+    near_ref, res, vec, own_mod, west, east, south, north, out, modulus, rows, coeff, first, second, scaled, shift
 ):
     modulus[2:10, 2:10, :] = own_mod[...]
     modulus[0:2, 2:10, :] = west[384:400, :].reshape(2, 8, 128)
@@ -325,12 +349,7 @@
         modulus[x, 10:12, :] = north[576 + 2 * x : 578 + 2 * x, :]
     sweep_rows(modulus, rows)
 
-    parts = []
-    for step_x in range(3):
-        for step_y in range(3):
-            start = pl.multiple_of(place[step_x * 3 + step_y], 8)
-            parts.append(found[pl.ds(start, 8), :])
-    near = jnp.concatenate(parts, axis=0)
+    near = near_ref[...]
     near = jnp.concatenate([near, jnp.zeros((72, 96), jnp.float32)], axis=1)
     near = jnp.concatenate([near, jnp.zeros((56, 128), jnp.float32)], axis=0)
     turned = near.T[:32]
@@ -352,7 +371,7 @@
         correct(4, (x + 2) * 12 + y + 2, vec, lambda k, c: (k * 3 + c) * 64 + index, False)
         return carry
 
-    lax.fori_loop(0, 64, own_cell, 0)
+    lax.fori_loop(0, 64, own_cell, 0, unroll=2)
 
     def edge_cells(y, carry):
         for layer in range(2):
@@ -379,7 +398,7 @@
         scale_cell(x + 1, y + 1, res, lambda c: c * 64 + index, 192)
         return carry
 
-    lax.fori_loop(0, 64, own_scaled, 0)
+    lax.fori_loop(0, 64, own_scaled, 0, unroll=4)
 
     def edge_scaled(y, carry):
         scale_cell(0, y + 1, west, lambda c: 400 + c * 8 + y, 24)
@@ -388,7 +407,7 @@
         scale_cell(y + 1, 9, north, lambda c: 600 + c * 8 + y, 24)
         return carry
 
-    lax.fori_loop(0, 8, edge_scaled, 0)
+    lax.fori_loop(0, 8, edge_scaled, 0, unroll=2)
 
     up = lax.broadcasted_iota(jnp.int32, (256, 256), 0) % 128
     to = lax.broadcasted_iota(jnp.int32, (256, 256), 1)
@@ -443,12 +462,12 @@
     lax.fori_loop(0, 8, last, 0)
 
 
-def local_parts(place, found, residuals, vectors, modulus, west, east, south, north):
+def local_parts(near, residuals, vectors, modulus, west, east, south, north):
     whole = pl.BlockSpec(memory_space=pltpu.VMEM)
     result = pl.pallas_call(
         local_stage,
         out_shape=jax.ShapeDtypeStruct((6144, 128), jnp.float32),
-        in_specs=[pl.BlockSpec(memory_space=pltpu.SMEM)] + [whole] * 8,
+        in_specs=[whole] * 8,
         out_specs=whole,
         scratch_shapes=[
             pltpu.VMEM((12, 16, 128), jnp.float32),
@@ -461,8 +480,7 @@
         ],
         compiler_params=pltpu.CompilerParams(vmem_limit_bytes=48 * 1024 * 1024),
     )(
-        place,
-        found,
+        near,
         residuals.reshape(6144, 128),
         vectors.reshape(1536, 128),
         modulus,
@@ -496,7 +514,7 @@
     modulus = jnp.sum(stiffness[:, None, None, None] * choose, axis=0)
     east_face = shifted(lines(vectors[:, :, 0], modulus[0]), "gx", -1)
     north_face = shifted(lines(vectors[:, :, :, 0], modulus[:, 0]), "yz", -1)
-    spot = index_y.astype(jnp.int32).reshape(1)
+    spot = jnp.stack([index_x, index_y]).astype(jnp.int32)
     every = coarse_rows(spot, residuals, vectors, modulus, east_face, north_face, count)
     to_west = lines(vectors[:, :, 0:2], modulus[0:2], residuals[:, :, 0])
     to_east = lines(vectors[:, :, 6:8], modulus[6:8], residuals[:, :, 7])
@@ -512,12 +530,8 @@
     )
     south = shifted(lines(wide_vectors[:, :, :, 6:8], wide_modulus[:, 6:8], residuals[:, :, :, 7]), "yz", 1)
     north = shifted(lines(wide_vectors[:, :, :, 0:2], wide_modulus[:, 0:2], residuals[:, :, :, 0]), "yz", -1)
-    coeffs_all = solve_rows(rows, count_x, count_y * width)
-    coeffs = lax.dynamic_slice_in_dim(coeffs_all, (index_x * count_y + index_y) * width, width, 0)
-    near_x = jnp.clip(index_x + jnp.arange(-1, 2), 0, count_x - 1)
-    near_y = jnp.clip(index_y + jnp.arange(-1, 2), 0, count_y - 1)
-    place = ((near_x[:, None] * count_y + near_y[None, :]) * width).reshape(9).astype(jnp.int32)
-    result = local_parts(place, coeffs_all, residuals, vectors, modulus, west, east, south, north)
+    coeffs, near = solve_rows(spot, rows, count_x, count_y * width)
+    result = local_parts(near, residuals, vectors, modulus, west, east, south, north)
     return (coeffs, result)
 
 

time: 120 us -> 114 us (0.950)
  Pallas kernels: 68.5 us -> 59 us
  local copies, waits for them, and re-layouts: 13.5 us -> 16.7 us
    pallas_call x1, Pallas kernels: 10.9 us -> 5.68 us  [coarse_rows(): pl.pallas_call(coarse_panel, out_shape=jax.ShapeDtypeStruct((count, 8, 12...]
    pallas_call x1, Pallas kernels: 7.66 us -> 4.19 us  [coarse_rows(): pl.pallas_call(project, out_shape=jax.ShapeDtypeStruct((8, 128), jnp.floa...]
    unnamed x16 -> x26, local copies, waits for them, and re-layouts: 3.8 us -> 6.97 us
    pallas_call x1, Pallas kernels: 27.1 us -> 25 us  [local_parts(): pl.pallas_call(local_stage, out_shape=jax.ShapeDtypeStruct((6144, 128), j...]
    pallas_call x1, Pallas kernels: 22.8 us -> 24.1 us  [solve_rows(): pl.pallas_call(functools.partial(coarse_solve, slabs, size, chunk), out_s...]
  transfers between devices with their start and end apart: 7 -> 7, of which waited for: 1 -> 1; matrix products, arithmetic and copies ran while one was open for 12% -> 12% of each run, Pallas kernels for 26% -> 25%
where the time goes in v2:
time: 114 us; the launch traced here: 113 us
  Pallas kernels  59 us (52%)
  starting transfers between devices  27.9 us (24%)
  local copies, waits for them, and re-layouts  16.7 us (15%)
  other arithmetic  6.26 us (5%)
  waiting for transfers between devices  2.23 us (2%)
    pallas_call x1, Pallas kernels, local_parts(): pl.pallas_call(local_stage, out_shape=jax.ShapeDtypeStruct((6144, 128), j...  25 us
    pallas_call x1, Pallas kernels, solve_rows(): pl.pallas_call(functools.partial(coarse_solve, slabs, size, chunk), out_s...  24.1 us
    ppermute x6, starting transfers between devices, shifted(): lax.ppermute(values, axis, [(i, i + step) for i in range(count) if 0 <= i...  14.5 us
    all_to_all x1, starting transfers between devices, on_device(): rows = lax.all_to_all(every, ('gx', 'yz'), 0, 0)  13.3 us
    unnamed x26, local copies, waits for them, and re-layouts  6.97 us
    pallas_call x1, Pallas kernels, coarse_rows(): pl.pallas_call(coarse_panel, out_shape=jax.ShapeDtypeStruct((count, 8, 12...  5.68 us
    pallas_call x1, Pallas kernels, coarse_rows(): pl.pallas_call(project, out_shape=jax.ShapeDtypeStruct((8, 128), jnp.floa...  4.19 us
    concatenate x5, other arithmetic, lines(): return jnp.concatenate([array.reshape(-1, 128) for array in arrays], axis=0)  3.59 us
  transfers between devices with their start and end apart: 7, of which 1 were waited for; matrix products, arithmetic and copies ran while one was open for 12% of the time, Pallas kernels for 25%

profile of v2, /device:TPU:1, one launch (start us, length us, event | category | flops | bytes accessed | tf_op | source)
XLA Modules:
  0.0 112.9 jit_solution(12647619588338954364)
XLA Ops:
  0.6 1.0 select_reduce_fusion.modulus.own_mod
  1.7 0.9 slice.60
  2.6 3.3 %collective-permute-start = (f32[200,128]{1,0:T(8,128)S(1)}, f32[200,128]{1,0:T(8,128)S(1)}, u32[]{:S(2)}, u32[]{:S(2)}) collective-permute-start(f32[200,128]{1,0:T(8,128)S(1)} %pad_maximum_fusion.7), channel_id=1, source_target_pairs={{4,0},{8,4},{12,8},{16,12},{20,16},{24,20},{28,24},{32,28},{36,32}... | collective-permute-start | bytes 307208 | tf_op jit(solution)/shard_map/ppermute | solution.py:496
  5.9 1.2 %slice.62 = f32[8,3,8,1,128]{4,3,2,1,0:T(1,128)S(1)} slice(f32[8,3,8,8,128]{4,3,2,1,0:T(8,128)} %param.5), slice={[0:8], [0:3], [0:8], [0:1], [0:128]} | slice | bytes 196608 | tf_op jit(solution)/shard_map/slice | solution.py:516
  7.8 1.3 %collective-permute-start.1 = (f32[200,128]{1,0:T(8,128)}, f32[200,128]{1,0:T(8,128)S(1)}, u32[]{:S(2)}, u32[]{:S(2)}) collective-permute-start(f32[200,128]{1,0:T(8,128)} %pad_maximum_fusion.8), channel_id=1, source_target_pairs={{1,0},{2,1},{3,2},{5,4},{6,5},{7,6},{9,8},{10,9},{11,10},{13,12},{... | collective-permute-start | bytes 307208 | tf_op jit(solution)/shard_map/ppermute | solution.py:496
  9.1 1.8 %fusion.2 = (f32[8,3,2,8,128]{4,3,2,1,0:T(8,128)}, f32[8,3,2,8,128]{4,3,2,1,0:T(8,128)}) fusion(f32[8,3,8,8,128]{4,3,2,1,0:T(8,128)} %param.5), kind=kLoop, calls=%fused_computation.22 | loop fusion | bytes 786432 | tf_op jit(solution)/shard_map/slice | solution.py:520
  10.9 1.2 %fusion.1 = (f32[32,3,1,8,128]{4,3,2,1,0:T(8,128)S(1)}, f32[32,3,1,8,128]{4,3,2,1,0:T(8,128)S(1)}) fusion(f32[32,3,8,8,128]{4,3,2,1,0:T(8,128)} %param.4), kind=kLoop, calls=%fused_computation.21 | loop fusion | bytes 1572864 | tf_op jit(solution)/shard_map/slice | solution.py:520
  12.1 1.1 copy-done.1
  13.2 4.2 %shard_map.59.known = f32[8,128]{1,0:T(8,128)S(1)} custom-call(f32[1536,128]{1,0:T(8,128)S(1)} %bitcast.34, f32[6144,128]{1,0:T(8,128)S(1)} %bitcast.33), custom_call_target="tpu_custom_call" | custom-call | flops 12600000 | bytes 4000000 | tf_op jit(solution)/shard_map/pallas_call | solution.py:297
  17.4 1.1 pad_maximum_fusion.2
  18.6 5.7 %shard_map.60 = f32[128,8,128]{2,1,0:T(8,128)S(1)} custom-call(s32[2]{0:T(128)S(1)} %pad_add_fusion.spot, f32[1536,128]{1,0:T(8,128)S(1)} %bitcast.35, f32[8,8,128]{2,1,0:T(8,128)S(1)} %select_reduce_fusion.modulus.own_mod, f32[200,128]{1,0:T(8,128)S(1)} %collective-permute-done.east, f32[200,128]{1,0:T(8,128)S(1)} %collective-permute-done.1.north, ...), custom_call_target="tpu_custom_call" | custom-call | flops 6000000 | bytes 2000000 | tf_op jit(solution)/shard_map/pallas_call | solution.py:305
  24.3 0.8 copy-done.4
  25.1 3.1 %collective-permute-start.2 = (f32[1168,128]{1,0:T(8,128)}, f32[1168,128]{1,0:T(8,128)}, u32[]{:S(2)}, u32[]{:S(2)}) collective-permute-start(f32[1168,128]{1,0:T(8,128)} %get-tuple-element.10), channel_id=1, source_target_pairs={{0,4},{4,8},{8,12},{12,16},{16,20},{20,24},{24,28},{28,32},{32,36}... | collective-permute-start | bytes 1794056 | tf_op jit(solution)/shard_map/ppermute | solution.py:496
  28.2 2.1 %collective-permute-start.3 = (f32[1168,128]{1,0:T(8,128)}, f32[1168,128]{1,0:T(8,128)}, u32[]{:S(2)}, u32[]{:S(2)}) collective-permute-start(f32[1168,128]{1,0:T(8,128)} %get-tuple-element.11), channel_id=1, source_target_pairs={{4,0},{8,4},{12,8},{16,12},{20,16},{24,20},{28,24},{32,28},{36,32}... | collective-permute-start | bytes 1794056 | tf_op jit(solution)/shard_map/ppermute | solution.py:496
  30.2 1.4 %fusion = (f32[32,3,8,1,128]{4,3,2,1,0:T(1,128)}, f32[32,3,8,1,128]{4,3,2,1,0:T(1,128)}) fusion(f32[32,3,8,8,128]{4,3,2,1,0:T(8,128)S(1)} %copy-done), kind=kLoop, calls=%fused_computation.20 | loop fusion | bytes 1572864 | tf_op jit(solution)/shard_map/slice | solution.py:532
  31.6 13.3 %all-to-all-start = ((f32[128,8,128]{2,1,0:T(8,128)}), f32[128,8,128]{2,1,0:T(8,128)S(1)}, u32[]{:S(2)}, u32[]{:S(2)}) async-start(f32[128,8,128]{2,1,0:T(8,128)} %copy-done.4), calls=%async_computation | async-start | bytes 1048576 | tf_op jit(solution)/shard_map/all_to_all | solution.py:522
  45.0 0.9 slice.84
  46.0 0.9 slice.85
  46.9 1.6 %pad_maximum_fusion.4 = (f32[8,3,12,2,128]{4,3,2,1,0:T(2,128)S(1)}, f32[8,3,12,2,128]{4,3,2,1,0:T(2,128)S(1)}) fusion(f32[8,3,2,8,128]{4,3,2,1,0:T(8,128)S(1)} %bitcast.45, f32[8,3,8,8,128]{4,3,2,1,0:T(8,128)} %param.5, f32[8,3,2,8,128]{4,3,2,1,0:T(8,128)S(1)} %bitcast.44), kind=kLoop, calls=%fused_computation.4 | loop fusion | flops 294912 | bytes 1769472 | tf_op jit(solution)/shard_map/concatenate | solution.py:525
  48.5 0.7 slice_bitcast_fusion.1
  49.9 0.9 pad_maximum_fusion
  50.8 3.3 %collective-permute-start.4 = (f32[1368,128]{1,0:T(8,128)}, f32[1368,128]{1,0:T(8,128)S(1)}, u32[]{:S(2)}, u32[]{:S(2)}) collective-permute-start(f32[1368,128]{1,0:T(8,128)} %pad_maximum_fusion), channel_id=1, source_target_pairs={{0,1},{1,2},{2,3},{4,5},{5,6},{6,7},{8,9},{9,10},{10,11},{12,13},{... | collective-permute-start | bytes 2101256 | tf_op jit(solution)/shard_map/ppermute | solution.py:496
  54.1 0.9 pad_maximum_fusion.1
  55.1 1.5 %collective-permute-start.5 = (f32[1368,128]{1,0:T(8,128)}, f32[1368,128]{1,0:T(8,128)S(1)}, u32[]{:S(2)}, u32[]{:S(2)}) collective-permute-start(f32[1368,128]{1,0:T(8,128)} %pad_maximum_fusion.1), channel_id=1, source_target_pairs={{1,0},{2,1},{3,2},{5,4},{6,5},{7,6},{9,8},{10,9},{11,10},{13,12},{... | collective-permute-start | bytes 2101256 | tf_op jit(solution)/shard_map/ppermute | solution.py:496
  56.5 2.2 %all-to-all-done.rows_ref = f32[128,8,128]{2,1,0:T(8,128)S(1)} async-done(((f32[128,8,128]{2,1,0:T(8,128)}), f32[128,8,128]{2,1,0:T(8,128)S(1)}, u32[]{:S(2)}, u32[]{:S(2)}) %all-to-all-start) | async-done | bytes 524320 | tf_op jit(solution)/shard_map/all_to_all | solution.py:522
  58.7 24.1 %shard_map.61 = (f32[8,32]{1,0:T(8,128)}, f32[72,32]{1,0:T(8,128)S(1)}) custom-call(s32[2]{0:T(128)S(1)} %pad_add_fusion.spot, f32[128,8,128]{2,1,0:T(8,128)S(1)} %all-to-all-done.rows_ref), custom_call_target="tpu_custom_call" | custom-call | flops 20000000000 | bytes 90000000 | tf_op jit(solution)/shard_map/pallas_call | solution.py:159
  82.9 0.8 copy-done.5
  83.8 0.8 copy-done.7
  84.6 1.1 %copy-done.3 = f32[8,3,8,8,128]{4,3,2,1,0:T(8,128)S(1)} copy-done((f32[8,3,8,8,128]{4,3,2,1,0:T(8,128)S(1)}, f32[8,3,8,8,128]{4,3,2,1,0:T(8,128)}, u32[]{:S(2)}) %copy-start.3) | copy-done | bytes 786456
  85.7 1.1 copy-done.6
  86.8 1.1 copy-done.8
  87.9 25.0 %shard_map.62 = f32[6144,128]{1,0:T(8,128)} custom-call(f32[72,32]{1,0:T(8,128)S(1)} %get-tuple-element.9.near_ref, f32[6144,128]{1,0:T(8,128)} %bitcast.32, f32[1536,128]{1,0:T(8,128)S(1)} %bitcast.36, f32[8,8,128]{2,1,0:T(8,128)S(1)} %select_reduce_fusion.modulus.own_mod, f32[1168,128]{1,0:T(8,128)} %collective-permute-done.2.west, ...), custom_call_target="tpu_custom_call" | custom-call | tf_op jit(solution)/shard_map/pallas_call | solution.py:467
  (33 shorter events, 1.5 us)
Async XLA Ops:
  0.6 11.4 %copy-start = (f32[32,3,8,8,128]{4,3,2,1,0:T(8,128)S(1)}, f32[32,3,8,8,128]{4,3,2,1,0:T(8,128)}, u32[]{:S(2)}) copy-start(f32[32,3,8,8,128]{4,3,2,1,0:T(8,128)} %param.4) | copy-start | bytes 9437188
  2.6 16.0 %collective-permute-start = (f32[200,128]{1,0:T(8,128)S(1)}, f32[200,128]{1,0:T(8,128)S(1)}, u32[]{:S(2)}, u32[]{:S(2)}) collective-permute-start(f32[200,128]{1,0:T(8,128)S(1)} %pad_maximum_fusion.7), channel_id=1, source_target_pairs={{4,0},{8,4},{12,8},{16,12},{20,16},{24,20},{28,24},{32,28},{36,32}... | collective-permute-start | bytes 307208 | tf_op jit(solution)/shard_map/ppermute | solution.py:496
  7.8 10.8 %collective-permute-start.1 = (f32[200,128]{1,0:T(8,128)}, f32[200,128]{1,0:T(8,128)S(1)}, u32[]{:S(2)}, u32[]{:S(2)}) collective-permute-start(f32[200,128]{1,0:T(8,128)} %pad_maximum_fusion.8), channel_id=1, source_target_pairs={{1,0},{2,1},{3,2},{5,4},{6,5},{7,6},{9,8},{10,9},{11,10},{13,12},{... | collective-permute-start | bytes 307208 | tf_op jit(solution)/shard_map/ppermute | solution.py:496
  12.1 1.1 %copy-start.1 = (f32[8,3,8,8,128]{4,3,2,1,0:T(8,128)S(1)}, f32[8,3,8,8,128]{4,3,2,1,0:T(8,128)}, u32[]{:S(2)}) copy-start(f32[8,3,8,8,128]{4,3,2,1,0:T(8,128)} %param.5) | copy-start | bytes 2359300
  13.2 4.2 %copy-start.11 = (f32[8,3,2,8,128]{4,3,2,1,0:T(8,128)S(1)}, f32[8,3,2,8,128]{4,3,2,1,0:T(8,128)}, u32[]{:S(2)}) copy-start(f32[8,3,2,8,128]{4,3,2,1,0:T(8,128)} %get-tuple-element.18) | copy-start | bytes 589828
  13.2 4.2 %copy-start.12 = (f32[8,3,2,8,128]{4,3,2,1,0:T(8,128)S(1)}, f32[8,3,2,8,128]{4,3,2,1,0:T(8,128)}, u32[]{:S(2)}) copy-start(f32[8,3,2,8,128]{4,3,2,1,0:T(8,128)} %get-tuple-element.19) | copy-start | bytes 589828
  13.2 5.4 %copy-start.2 = (f32[8,3,8,8,128]{4,3,2,1,0:T(8,128)S(1)}, f32[8,3,8,8,128]{4,3,2,1,0:T(8,128)}, u32[]{:S(2)}) copy-start(f32[8,3,8,8,128]{4,3,2,1,0:T(8,128)} %param.5) | copy-start | bytes 2359300
  24.3 0.8 copy-start.4
  25.1 19.9 %collective-permute-start.2 = (f32[1168,128]{1,0:T(8,128)}, f32[1168,128]{1,0:T(8,128)}, u32[]{:S(2)}, u32[]{:S(2)}) collective-permute-start(f32[1168,128]{1,0:T(8,128)} %get-tuple-element.10), channel_id=1, source_target_pairs={{0,4},{4,8},{8,12},{12,16},{16,20},{20,24},{24,28},{28,32},{32,36}... | collective-permute-start | bytes 1794056 | tf_op jit(solution)/shard_map/ppermute | solution.py:496
  28.2 17.8 %collective-permute-start.3 = (f32[1168,128]{1,0:T(8,128)}, f32[1168,128]{1,0:T(8,128)}, u32[]{:S(2)}, u32[]{:S(2)}) collective-permute-start(f32[1168,128]{1,0:T(8,128)} %get-tuple-element.11), channel_id=1, source_target_pairs={{4,0},{8,4},{12,8},{16,12},{20,16},{24,20},{28,24},{32,28},{36,32}... | collective-permute-start | bytes 1794056 | tf_op jit(solution)/shard_map/ppermute | solution.py:496
  31.6 18.2 %copy-start.10 = (f32[32,3,8,1,128]{4,3,2,1,0:T(1,128)S(1)}, f32[32,3,8,1,128]{4,3,2,1,0:T(1,128)}, u32[]{:S(2)}) copy-start(f32[32,3,8,1,128]{4,3,2,1,0:T(1,128)} %get-tuple-element.13) | copy-start | bytes 1179652
  31.6 22.5 %copy-start.9 = (f32[32,3,8,1,128]{4,3,2,1,0:T(1,128)S(1)}, f32[32,3,8,1,128]{4,3,2,1,0:T(1,128)}, u32[]{:S(2)}) copy-start(f32[32,3,8,1,128]{4,3,2,1,0:T(1,128)} %get-tuple-element.12) | copy-start | bytes 1179652
  31.6 27.1 %all-to-all-start = ((f32[128,8,128]{2,1,0:T(8,128)}), f32[128,8,128]{2,1,0:T(8,128)S(1)}, u32[]{:S(2)}, u32[]{:S(2)}) async-start(f32[128,8,128]{2,1,0:T(8,128)} %copy-done.4), calls=%async_computation | async-start | bytes 1048576 | tf_op jit(solution)/shard_map/all_to_all | solution.py:522
  50.8 32.1 %collective-permute-start.4 = (f32[1368,128]{1,0:T(8,128)}, f32[1368,128]{1,0:T(8,128)S(1)}, u32[]{:S(2)}, u32[]{:S(2)}) collective-permute-start(f32[1368,128]{1,0:T(8,128)} %pad_maximum_fusion), channel_id=1, source_target_pairs={{0,1},{1,2},{2,3},{4,5},{5,6},{6,7},{8,9},{9,10},{10,11},{12,13},{... | collective-permute-start | bytes 2101256 | tf_op jit(solution)/shard_map/ppermute | solution.py:496
  55.1 28.7 %collective-permute-start.5 = (f32[1368,128]{1,0:T(8,128)}, f32[1368,128]{1,0:T(8,128)S(1)}, u32[]{:S(2)}, u32[]{:S(2)}) collective-permute-start(f32[1368,128]{1,0:T(8,128)} %pad_maximum_fusion.1), channel_id=1, source_target_pairs={{1,0},{2,1},{3,2},{5,4},{6,5},{7,6},{9,8},{10,9},{11,10},{13,12},{... | collective-permute-start | bytes 2101256 | tf_op jit(solution)/shard_map/ppermute | solution.py:496
  82.9 0.9 copy-start.5
  83.8 0.8 copy-start.7
  84.6 1.1 %copy-start.3 = (f32[8,3,8,8,128]{4,3,2,1,0:T(8,128)S(1)}, f32[8,3,8,8,128]{4,3,2,1,0:T(8,128)}, u32[]{:S(2)}) copy-start(f32[8,3,8,8,128]{4,3,2,1,0:T(8,128)} %param.5) | copy-start | bytes 2359300
  85.7 1.1 copy-start.6
  86.8 1.1 copy-start.8

commit v3 on v2

--- a/solution.py
+++ b/solution.py
@@ -339,15 +339,13 @@
 
 
 def local_stage(
-    near_ref, res, vec, own_mod, west, east, south, north, out, modulus, rows, coeff, first, second, scaled, shift
+    near_ref, res_far, vec, own_mod, west_far, east_far, south_far, north_far, out_far,
+    modulus, rows, coeff, first, second, scaled, shift, res, west, east, south, north, out, arrived, left,
 ):
-    modulus[2:10, 2:10, :] = own_mod[...]
-    modulus[0:2, 2:10, :] = west[384:400, :].reshape(2, 8, 128)
-    modulus[10:12, 2:10, :] = east[384:400, :].reshape(2, 8, 128)
-    for x in range(12):
-        modulus[x, 0:2, :] = south[576 + 2 * x : 578 + 2 * x, :]
-        modulus[x, 10:12, :] = north[576 + 2 * x : 578 + 2 * x, :]
-    sweep_rows(modulus, rows)
+    pairs = ((west_far, west), (east_far, east), (south_far, south), (north_far, north), (res_far, res))
+    loads = [pltpu.make_async_copy(far, here, arrived.at[n]) for n, (far, here) in enumerate(pairs)]
+    for load in loads:
+        load.start()
 
     near = near_ref[...]
     near = jnp.concatenate([near, jnp.zeros((72, 96), jnp.float32)], axis=1)
@@ -373,18 +371,33 @@
 
     lax.fori_loop(0, 64, own_cell, 0, unroll=2)
 
+    for index in range(4):
+        loads[index].wait()
+    modulus[...] = jnp.zeros(modulus.shape, jnp.float32)
+    modulus[2:10, 2:10, :] = own_mod[...]
+    modulus[0:2, 2:10, :] = west[384:400, :].reshape(2, 8, 128)
+    modulus[10:12, 2:10, :] = east[384:400, :].reshape(2, 8, 128)
+    for x in range(8):
+        modulus[x + 2, 0:2, :] = south[384 + 2 * x : 386 + 2 * x, :]
+        modulus[x + 2, 10:12, :] = north[384 + 2 * x : 386 + 2 * x, :]
+    for y, side in ((1, south), (10, north)):
+        modulus[1, y : y + 1, :] = side[1192:1193, :]
+        modulus[10, y : y + 1, :] = side[1217:1218, :]
+    sweep_rows(modulus, rows)
+
     def edge_cells(y, carry):
         for layer in range(2):
             correct(1, layer * 12 + y + 2, west, lambda k, c: ((k * 3 + c) * 2 + layer) * 8 + y, layer == 0)
             correct(7, (10 + layer) * 12 + y + 2, east, lambda k, c: ((k * 3 + c) * 2 + layer) * 8 + y, layer == 1)
-            correct(3, (y + 2) * 12 + layer, south, lambda k, c: ((k * 3 + c) * 12 + y + 2) * 2 + layer, layer == 0)
-            correct(5, (y + 2) * 12 + 10 + layer, north, lambda k, c: ((k * 3 + c) * 12 + y + 2) * 2 + layer, layer == 1)
+            correct(3, (y + 2) * 12 + layer, south, lambda k, c: ((k * 3 + c) * 8 + y) * 2 + layer, layer == 0)
+            correct(5, (y + 2) * 12 + 10 + layer, north, lambda k, c: ((k * 3 + c) * 8 + y) * 2 + layer, layer == 1)
         return carry
 
     lax.fori_loop(0, 8, edge_cells, 0)
-    for x, near_x in ((1, 0), (10, 6)):
-        correct(near_x, x * 12 + 1, south, lambda k, c: ((k * 3 + c) * 12 + x) * 2 + 1, True)
-        correct(near_x + 2, x * 12 + 10, north, lambda k, c: ((k * 3 + c) * 12 + x) * 2, True)
+    for x, near_x, start in ((1, 0, 1168), (10, 6, 1193)):
+        correct(near_x, x * 12 + 1, south, lambda k, c: start + k * 3 + c, True)
+        correct(near_x + 2, x * 12 + 10, north, lambda k, c: start + k * 3 + c, True)
+    loads[4].wait()
 
     def scale_cell(x, y, source, start, stride):
         weight = rows[6, x, pl.ds(y, 1), :]
@@ -403,8 +416,8 @@
     def edge_scaled(y, carry):
         scale_cell(0, y + 1, west, lambda c: 400 + c * 8 + y, 24)
         scale_cell(9, y + 1, east, lambda c: 400 + c * 8 + y, 24)
-        scale_cell(y + 1, 0, south, lambda c: 600 + c * 8 + y, 24)
-        scale_cell(y + 1, 9, north, lambda c: 600 + c * 8 + y, 24)
+        scale_cell(y + 1, 0, south, lambda c: 400 + c * 8 + y, 24)
+        scale_cell(y + 1, 9, north, lambda c: 400 + c * 8 + y, 24)
         return carry
 
     lax.fori_loop(0, 8, edge_scaled, 0, unroll=2)
@@ -457,18 +470,24 @@
                     out[pl.ds(comp * 64 + x * 8 + y + n, 32, stride=192), :] = value[comp * 32 : comp * 32 + 32]
 
             relax(x + 1, y + 1, 4, second, keep)
-        return carry
+        slab(x).start()
+        return carry
+
+    def slab(x):
+        return pltpu.make_async_copy(out.reshape(96, 8, 8, 128).at[:, x], out_far.at[:, x], left.at[x])
 
     lax.fori_loop(0, 8, last, 0)
+    for x in range(8):
+        slab(x).wait()
 
 
 def local_parts(near, residuals, vectors, modulus, west, east, south, north):
-    whole = pl.BlockSpec(memory_space=pltpu.VMEM)
+    whole, far = pl.BlockSpec(memory_space=pltpu.VMEM), pl.BlockSpec(memory_space=pl.ANY)
     result = pl.pallas_call(
         local_stage,
-        out_shape=jax.ShapeDtypeStruct((6144, 128), jnp.float32),
-        in_specs=[whole] * 8,
-        out_specs=whole,
+        out_shape=jax.ShapeDtypeStruct((96, 8, 8, 128), jnp.float32),
+        in_specs=[whole, far, whole, whole, far, far, far, far],
+        out_specs=far,
         scratch_shapes=[
             pltpu.VMEM((12, 16, 128), jnp.float32),
             pltpu.VMEM((7, 10, 16, 128), jnp.float32),
@@ -477,8 +496,16 @@
             pltpu.VMEM((144, 96, 128), jnp.float32),
             pltpu.VMEM((100, 96, 128), jnp.float32),
             pltpu.VMEM((256, 256), jnp.bfloat16),
+            pltpu.VMEM((6144, 128), jnp.float32),
+            pltpu.VMEM((1168, 128), jnp.float32),
+            pltpu.VMEM((1168, 128), jnp.float32),
+            pltpu.VMEM((1218, 128), jnp.float32),
+            pltpu.VMEM((1218, 128), jnp.float32),
+            pltpu.VMEM((6144, 128), jnp.float32),
+            pltpu.SemaphoreType.DMA((5,)),
+            pltpu.SemaphoreType.DMA((8,)),
         ],
-        compiler_params=pltpu.CompilerParams(vmem_limit_bytes=48 * 1024 * 1024),
+        compiler_params=pltpu.CompilerParams(vmem_limit_bytes=58 * 1024 * 1024),
     )(
         near,
         residuals.reshape(6144, 128),
@@ -522,14 +549,16 @@
     rows = lax.all_to_all(every, ("gx", "yz"), 0, 0)
     west = shifted(to_east, "gx", 1)
     east = shifted(to_west, "gx", -1)
-    wide_vectors = jnp.concatenate(
-        [west[:384].reshape(8, 3, 2, 8, 128), vectors, east[:384].reshape(8, 3, 2, 8, 128)], axis=2
+    south = shifted(
+        lines(vectors[:, :, :, 6:8], modulus[:, 6:8], residuals[:, :, :, 7], west[15:400:16], east[7:400:16]),
+        "yz",
+        1,
     )
-    wide_modulus = jnp.concatenate(
-        [west[384:400].reshape(2, 8, 128), modulus, east[384:400].reshape(2, 8, 128)], axis=0
+    north = shifted(
+        lines(vectors[:, :, :, 0:2], modulus[:, 0:2], residuals[:, :, :, 0], west[8:400:16], east[0:400:16]),
+        "yz",
+        -1,
     )
-    south = shifted(lines(wide_vectors[:, :, :, 6:8], wide_modulus[:, 6:8], residuals[:, :, :, 7]), "yz", 1)
-    north = shifted(lines(wide_vectors[:, :, :, 0:2], wide_modulus[:, 0:2], residuals[:, :, :, 0]), "yz", -1)
     coeffs, near = solve_rows(spot, rows, count_x, count_y * width)
     result = local_parts(near, residuals, vectors, modulus, west, east, south, north)
     return (coeffs, result)

time: 114 us -> 109 us (0.956)
  other arithmetic: 6.26 us -> 2.86 us
  waiting for transfers between devices: 2.23 us -> 0.02 us
  local copies, waits for them, and re-layouts: 16.7 us -> 18 us
    concatenate x0 -> x2, local copies, waits for them, and re-layouts: none -> 3.39 us  [lines(): return jnp.concatenate([array.reshape(-1, 128) for array in arrays], axis=0)]
    unnamed x26 -> x20, local copies, waits for them, and re-layouts: 6.97 us -> 3.58 us
    slice x2 -> x6, local copies, waits for them, and re-layouts: 1.88 us -> 4.59 us  [the longest x1 0.95 us: on_device(): east[7:400:16]]
    all_to_all x1, waiting for transfers between devices: 2.22 us -> 0.01 us  [on_device(): rows = lax.all_to_all(every, ('gx', 'yz'), 0, 0)]
    concatenate x5 -> x3, other arithmetic: 3.59 us -> 1.77 us  [lines(): return jnp.concatenate([array.reshape(-1, 128) for array in arrays], axis=0)]
    pallas_call x1, Pallas kernels: 25 us -> 23.3 us  [local_parts(): pl.pallas_call(local_stage, out_shape=jax.ShapeDtypeStruct((96, 8, 8, 128...]
    concatenate x2 -> x0, other arithmetic: 1.58 us -> none  [the longest x1 1.57 us: on_device(): jnp.concatenate([west[:384].reshape(8, 3, 2, 8, 128), vectors, east[:384]...]
    reshape x2 -> x0, local copies, waits for them, and re-layouts: 1.4 us -> none  [the longest x1 0.7 us: on_device(): west[384:400].reshape(2, 8, 128)]
  transfers between devices with their start and end apart: 7 -> 7, of which waited for: 1 -> 0; matrix products, arithmetic and copies ran while one was open for 12% -> 14% of each run, Pallas kernels for 25% -> 27%
where the time goes in v3:
time: 109 us; the launch traced here: 108 us
  Pallas kernels  57.9 us (53%)
  starting transfers between devices  28.4 us (26%)
  local copies, waits for them, and re-layouts  18 us (17%)
  other arithmetic  2.86 us (3%)
    pallas_call x1, Pallas kernels, solve_rows(): pl.pallas_call(functools.partial(coarse_solve, slabs, size, chunk), out_s...  24.7 us
    pallas_call x1, Pallas kernels, local_parts(): pl.pallas_call(local_stage, out_shape=jax.ShapeDtypeStruct((96, 8, 8, 128...  23.3 us
    ppermute x6, starting transfers between devices, shifted(): lax.ppermute(values, axis, [(i, i + step) for i in range(count) if 0 <= i...  14.6 us
    all_to_all x1, starting transfers between devices, on_device(): rows = lax.all_to_all(every, ('gx', 'yz'), 0, 0)  13.8 us
    pallas_call x1, Pallas kernels, coarse_rows(): pl.pallas_call(coarse_panel, out_shape=jax.ShapeDtypeStruct((count, 8, 12...  5.68 us
    pallas_call x1, Pallas kernels, coarse_rows(): pl.pallas_call(project, out_shape=jax.ShapeDtypeStruct((8, 128), jnp.floa...  4.22 us
    unnamed x20, local copies, waits for them, and re-layouts  3.58 us
    concatenate x2, local copies, waits for them, and re-layouts, lines(): return jnp.concatenate([array.reshape(-1, 128) for array in arrays], axis=0)  3.39 us
  transfers between devices with their start and end apart: 7, of which 0 were waited for; matrix products, arithmetic and copies ran while one was open for 14% of the time, Pallas kernels for 27%

profile of v3, /device:TPU:1, one launch (start us, length us, event | category | flops | bytes accessed | tf_op | source)
XLA Modules:
  0.0 108.2 jit_solution(3889479680293769747)
XLA Ops:
  0.6 1.0 select_reduce_fusion.modulus.own_mod
  1.7 0.9 slice.60
  2.6 3.3 %collective-permute-start = (f32[200,128]{1,0:T(8,128)S(1)}, f32[200,128]{1,0:T(8,128)S(1)}, u32[]{:S(2)}, u32[]{:S(2)}) collective-permute-start(f32[200,128]{1,0:T(8,128)S(1)} %pad_maximum_fusion.2), channel_id=1, source_target_pairs={{4,0},{8,4},{12,8},{16,12},{20,16},{24,20},{28,24},{32,28},{36,32}... | collective-permute-start | bytes 307208 | tf_op jit(solution)/shard_map/ppermute | solution.py:523
  6.0 1.2 %slice.62 = f32[8,3,8,1,128]{4,3,2,1,0:T(1,128)S(1)} slice(f32[8,3,8,8,128]{4,3,2,1,0:T(8,128)} %param.5), slice={[0:8], [0:3], [0:8], [0:1], [0:128]} | slice | bytes 196608 | tf_op jit(solution)/shard_map/slice | solution.py:543
  7.1 0.6 pad_maximum_fusion.3
  7.8 1.3 %collective-permute-start.1 = (f32[200,128]{1,0:T(8,128)}, f32[200,128]{1,0:T(8,128)S(1)}, u32[]{:S(2)}, u32[]{:S(2)}) collective-permute-start(f32[200,128]{1,0:T(8,128)} %pad_maximum_fusion.3), channel_id=1, source_target_pairs={{1,0},{2,1},{3,2},{5,4},{6,5},{7,6},{9,8},{10,9},{11,10},{13,12},{... | collective-permute-start | bytes 307208 | tf_op jit(solution)/shard_map/ppermute | solution.py:523
  9.1 1.8 %fusion.3 = (f32[8,3,2,8,128]{4,3,2,1,0:T(8,128)}, f32[8,3,2,8,128]{4,3,2,1,0:T(8,128)}) fusion(f32[8,3,8,8,128]{4,3,2,1,0:T(8,128)} %param.5), kind=kLoop, calls=%fused_computation.13 | loop fusion | bytes 786432 | tf_op jit(solution)/shard_map/slice | solution.py:547
  10.9 1.2 %fusion.1 = (f32[32,3,1,8,128]{4,3,2,1,0:T(8,128)S(1)}, f32[32,3,1,8,128]{4,3,2,1,0:T(8,128)S(1)}) fusion(f32[32,3,8,8,128]{4,3,2,1,0:T(8,128)} %param.4), kind=kLoop, calls=%fused_computation.11 | loop fusion | bytes 1572864 | tf_op jit(solution)/shard_map/slice | solution.py:547
  12.1 1.1 %copy-done.1 = f32[8,3,8,8,128]{4,3,2,1,0:T(8,128)S(1)} copy-done((f32[8,3,8,8,128]{4,3,2,1,0:T(8,128)S(1)}, f32[8,3,8,8,128]{4,3,2,1,0:T(8,128)}, u32[]{:S(2)}) %copy-start.1) | copy-done | bytes 786456
  13.2 4.2 %shard_map.59.known = f32[8,128]{1,0:T(8,128)S(1)} custom-call(f32[1536,128]{1,0:T(8,128)S(1)} %bitcast.29, f32[6144,128]{1,0:T(8,128)S(1)} %bitcast.27), custom_call_target="tpu_custom_call" | custom-call | flops 12600000 | bytes 4000000 | tf_op jit(solution)/shard_map/pallas_call | solution.py:297
  17.4 1.1 %pad_maximum_fusion = (f32[1168,128]{1,0:T(8,128)}, f32[1168,128]{1,0:T(8,128)}) fusion(f32[768,128]{1,0:T(8,128)S(1)} %bitcast.35, f32[16,128]{1,0:T(8,128)S(1)} %get-tuple-element.23, f32[384,128]{1,0:T(8,128)S(1)} %bitcast.38, f32[768,128]{1,0:T(8,128)S(1)} %bitcast.34, f32[16,128]{1,0:T(8,128)S(1)} %get-tuple-element.22, f32[384,128]{1,0:T(8,128)S(1)} %bitcast.37), kind=kLoop, calls=%fused_computation | loop fusion | flops 598016 | bytes 2392064 | tf_op jit(solution)/shard_map/concatenate | solution.py:527
  18.6 0.1 pad_add_fusion.spot
  18.6 5.7 %shard_map.60 = f32[128,8,128]{2,1,0:T(8,128)S(1)} custom-call(s32[2]{0:T(128)S(1)} %pad_add_fusion.spot, f32[1536,128]{1,0:T(8,128)S(1)} %bitcast.30, f32[8,8,128]{2,1,0:T(8,128)S(1)} %select_reduce_fusion.modulus.own_mod, f32[200,128]{1,0:T(8,128)S(1)} %collective-permute-done.east, f32[200,128]{1,0:T(8,128)S(1)} %collective-permute-done.1.north, ...), custom_call_target="tpu_custom_call" | custom-call | flops 6000000 | bytes 2000000 | tf_op jit(solution)/shard_map/pallas_call | solution.py:305
  24.3 0.8 copy-done.3
  25.1 3.1 %collective-permute-start.2 = (f32[1168,128]{1,0:T(8,128)}, f32[1168,128]{1,0:T(8,128)}, u32[]{:S(2)}, u32[]{:S(2)}) collective-permute-start(f32[1168,128]{1,0:T(8,128)} %get-tuple-element.10), channel_id=1, source_target_pairs={{0,4},{4,8},{8,12},{12,16},{16,20},{20,24},{24,28},{28,32},{32,36}... | collective-permute-start | bytes 1794056 | tf_op jit(solution)/shard_map/ppermute | solution.py:523
  28.2 2.1 %collective-permute-start.3 = (f32[1168,128]{1,0:T(8,128)}, f32[1168,128]{1,0:T(8,128)}, u32[]{:S(2)}, u32[]{:S(2)}) collective-permute-start(f32[1168,128]{1,0:T(8,128)} %get-tuple-element.11), channel_id=1, source_target_pairs={{4,0},{8,4},{12,8},{16,12},{20,16},{24,20},{28,24},{32,28},{36,32}... | collective-permute-start | bytes 1794056 | tf_op jit(solution)/shard_map/ppermute | solution.py:523
  30.3 0.8 fusion.2
  31.1 13.8 %all-to-all-start = ((f32[128,8,128]{2,1,0:T(8,128)}), f32[128,8,128]{2,1,0:T(8,128)}, u32[]{:S(2)}, u32[]{:S(2)}) async-start(f32[128,8,128]{2,1,0:T(8,128)} %copy-done.3), calls=%async_computation | async-start | bytes 1048576 | tf_op jit(solution)/shard_map/all_to_all | solution.py:549
  44.9 1.4 %fusion = (f32[32,3,8,1,128]{4,3,2,1,0:T(1,128)}, f32[32,3,8,1,128]{4,3,2,1,0:T(1,128)}) fusion(f32[32,3,8,8,128]{4,3,2,1,0:T(8,128)S(1)} %copy-done), kind=kLoop, calls=%fused_computation.10 | loop fusion | bytes 1572864 | tf_op jit(solution)/shard_map/slice | solution.py:558
  46.3 0.9 slice.73
  47.3 0.9 slice.74
  48.2 2.2 %concatenate.22 = f32[1218,128]{1,0:T(8,128)S(1)} concatenate(f32[384,128]{1,0:T(8,128)} %bitcast.39, f32[16,128]{1,0:T(8,128)S(1)} %bitcast.43, f32[768,128]{1,0:T(8,128)} %bitcast.33, f32[25,128]{1,0:T(8,128)S(1)} %slice.73, f32[25,128]{1,0:T(8,128)S(1)} %slice.74), dimensions={0} | concatenate | bytes 1247232 | tf_op jit(solution)/shard_map/concatenate | solution.py:527
  50.4 3.3 %collective-permute-start.4 = (f32[1218,128]{1,0:T(8,128)S(1)}, f32[1218,128]{1,0:T(8,128)S(1)}, u32[]{:S(2)}, u32[]{:S(2)}) collective-permute-start(f32[1218,128]{1,0:T(8,128)S(1)} %concatenate.22), channel_id=1, source_target_pairs={{0,1},{1,2},{2,3},{4,5},{5,6},{6,7},{8,9},{9,10},{10,11},{12,13},{... | collective-permute-start | bytes 1870856 | tf_op jit(solution)/shard_map/ppermute | solution.py:523
  53.7 0.9 slice.78
  54.7 0.9 slice.79
  55.6 1.2 %concatenate.23 = f32[1218,128]{1,0:T(8,128)S(1)} concatenate(f32[384,128]{1,0:T(8,128)S(1)} %bitcast.36, f32[16,128]{1,0:T(8,128)S(1)} %bitcast.42, f32[768,128]{1,0:T(8,128)} %bitcast.32, f32[25,128]{1,0:T(8,128)S(1)} %slice.78, f32[25,128]{1,0:T(8,128)S(1)} %slice.79), dimensions={0} | concatenate | bytes 1247232 | tf_op jit(solution)/shard_map/concatenate | solution.py:527
  56.9 1.5 %collective-permute-start.5 = (f32[1218,128]{1,0:T(8,128)S(1)}, f32[1218,128]{1,0:T(8,128)S(1)}, u32[]{:S(2)}, u32[]{:S(2)}) collective-permute-start(f32[1218,128]{1,0:T(8,128)S(1)} %concatenate.23), channel_id=1, source_target_pairs={{1,0},{2,1},{3,2},{5,4},{6,5},{7,6},{9,8},{10,9},{11,10},{13,12},{... | collective-permute-start | bytes 1870856 | tf_op jit(solution)/shard_map/ppermute | solution.py:523
  58.4 24.7 %shard_map.61 = (f32[8,32]{1,0:T(8,128)}, f32[72,32]{1,0:T(8,128)S(1)}) custom-call(s32[2]{0:T(128)S(1)} %pad_add_fusion.spot, f32[128,8,128]{2,1,0:T(8,128)} %all-to-all-done.rows_ref), custom_call_target="tpu_custom_call" | custom-call | flops 20000000000 | bytes 90000000 | tf_op jit(solution)/shard_map/pallas_call | solution.py:159
  83.0 0.6 copy-done.5
  83.6 0.8 copy-done.8
  84.4 0.2 copy-done.9
  84.7 23.3 %shard_map.62 = f32[96,8,8,128]{3,2,1,0:T(8,128)} custom-call(f32[72,32]{1,0:T(8,128)} %copy-done.5, f32[6144,128]{1,0:T(8,128)} %bitcast.26, f32[1536,128]{1,0:T(8,128)} %bitcast.28, f32[8,8,128]{2,1,0:T(8,128)} %copy-done.4, f32[1168,128]{1,0:T(8,128)} %collective-permute-done.2.west_far, f32[1168,128]{1,0:T(8,128)} %collective-permute-done.3.east_far, ...), custom_call_target="tpu_custom_call" | custom-call | tf_op jit(solution)/shard_map/pallas_call | solution.py:486
  (27 shorter events, 0.1 us)
Async XLA Ops:
  0.6 11.4 %copy-start = (f32[32,3,8,8,128]{4,3,2,1,0:T(8,128)S(1)}, f32[32,3,8,8,128]{4,3,2,1,0:T(8,128)}, u32[]{:S(2)}) copy-start(f32[32,3,8,8,128]{4,3,2,1,0:T(8,128)} %param.4) | copy-start | bytes 9437188
  1.7 43.2 %copy-start.4 = (f32[8,8,128]{2,1,0:T(8,128)}, f32[8,8,128]{2,1,0:T(8,128)S(1)}, u32[]{:S(2)}) copy-start(f32[8,8,128]{2,1,0:T(8,128)S(1)} %select_reduce_fusion.modulus.own_mod) | copy-start | bytes 98308
  2.6 16.0 %collective-permute-start = (f32[200,128]{1,0:T(8,128)S(1)}, f32[200,128]{1,0:T(8,128)S(1)}, u32[]{:S(2)}, u32[]{:S(2)}) collective-permute-start(f32[200,128]{1,0:T(8,128)S(1)} %pad_maximum_fusion.2), channel_id=1, source_target_pairs={{4,0},{8,4},{12,8},{16,12},{20,16},{24,20},{28,24},{32,28},{36,32}... | collective-permute-start | bytes 307208 | tf_op jit(solution)/shard_map/ppermute | solution.py:523
  7.8 10.9 %collective-permute-start.1 = (f32[200,128]{1,0:T(8,128)}, f32[200,128]{1,0:T(8,128)S(1)}, u32[]{:S(2)}, u32[]{:S(2)}) collective-permute-start(f32[200,128]{1,0:T(8,128)} %pad_maximum_fusion.3), channel_id=1, source_target_pairs={{1,0},{2,1},{3,2},{5,4},{6,5},{7,6},{9,8},{10,9},{11,10},{13,12},{... | collective-permute-start | bytes 307208 | tf_op jit(solution)/shard_map/ppermute | solution.py:523
  12.1 1.1 %copy-start.1 = (f32[8,3,8,8,128]{4,3,2,1,0:T(8,128)S(1)}, f32[8,3,8,8,128]{4,3,2,1,0:T(8,128)}, u32[]{:S(2)}) copy-start(f32[8,3,8,8,128]{4,3,2,1,0:T(8,128)} %param.5) | copy-start | bytes 2359300
  13.2 4.2 %copy-start.6 = (f32[8,3,2,8,128]{4,3,2,1,0:T(8,128)S(1)}, f32[8,3,2,8,128]{4,3,2,1,0:T(8,128)}, u32[]{:S(2)}) copy-start(f32[8,3,2,8,128]{4,3,2,1,0:T(8,128)} %get-tuple-element.18) | copy-start | bytes 589828
  13.2 4.2 %copy-start.7 = (f32[8,3,2,8,128]{4,3,2,1,0:T(8,128)S(1)}, f32[8,3,2,8,128]{4,3,2,1,0:T(8,128)}, u32[]{:S(2)}) copy-start(f32[8,3,2,8,128]{4,3,2,1,0:T(8,128)} %get-tuple-element.19) | copy-start | bytes 589828
  13.2 5.4 %copy-start.2 = (f32[8,3,8,8,128]{4,3,2,1,0:T(8,128)S(1)}, f32[8,3,8,8,128]{4,3,2,1,0:T(8,128)}, u32[]{:S(2)}) copy-start(f32[8,3,8,8,128]{4,3,2,1,0:T(8,128)} %param.5) | copy-start | bytes 2359300
  24.3 0.8 copy-start.3
  25.1 21.2 %collective-permute-start.2 = (f32[1168,128]{1,0:T(8,128)}, f32[1168,128]{1,0:T(8,128)}, u32[]{:S(2)}, u32[]{:S(2)}) collective-permute-start(f32[1168,128]{1,0:T(8,128)} %get-tuple-element.10), channel_id=1, source_target_pairs={{0,4},{4,8},{8,12},{12,16},{16,20},{20,24},{24,28},{28,32},{32,36}... | collective-permute-start | bytes 1794056 | tf_op jit(solution)/shard_map/ppermute | solution.py:523
  28.2 19.1 %collective-permute-start.3 = (f32[1168,128]{1,0:T(8,128)}, f32[1168,128]{1,0:T(8,128)}, u32[]{:S(2)}, u32[]{:S(2)}) collective-permute-start(f32[1168,128]{1,0:T(8,128)} %get-tuple-element.11), channel_id=1, source_target_pairs={{4,0},{8,4},{12,8},{16,12},{20,16},{24,20},{28,24},{32,28},{36,32}... | collective-permute-start | bytes 1794056 | tf_op jit(solution)/shard_map/ppermute | solution.py:523
  31.1 27.3 %all-to-all-start = ((f32[128,8,128]{2,1,0:T(8,128)}), f32[128,8,128]{2,1,0:T(8,128)}, u32[]{:S(2)}, u32[]{:S(2)}) async-start(f32[128,8,128]{2,1,0:T(8,128)} %copy-done.3), calls=%async_computation | async-start | bytes 1048576 | tf_op jit(solution)/shard_map/all_to_all | solution.py:549
  50.4 33.2 %collective-permute-start.4 = (f32[1218,128]{1,0:T(8,128)S(1)}, f32[1218,128]{1,0:T(8,128)S(1)}, u32[]{:S(2)}, u32[]{:S(2)}) collective-permute-start(f32[1218,128]{1,0:T(8,128)S(1)} %concatenate.22), channel_id=1, source_target_pairs={{0,1},{1,2},{2,3},{4,5},{5,6},{6,7},{8,9},{9,10},{10,11},{12,13},{... | collective-permute-start | bytes 1870856 | tf_op jit(solution)/shard_map/ppermute | solution.py:523
  56.9 26.8 %collective-permute-start.5 = (f32[1218,128]{1,0:T(8,128)S(1)}, f32[1218,128]{1,0:T(8,128)S(1)}, u32[]{:S(2)}, u32[]{:S(2)}) collective-permute-start(f32[1218,128]{1,0:T(8,128)S(1)} %concatenate.23), channel_id=1, source_target_pairs={{1,0},{2,1},{3,2},{5,4},{6,5},{7,6},{9,8},{10,9},{11,10},{13,12},{... | collective-permute-start | bytes 1870856 | tf_op jit(solution)/shard_map/ppermute | solution.py:523
  83.0 0.6 copy-start.5
  83.6 0.8 copy-start.8
  83.6 1.1 copy-start.9

commit v4 on v3

--- a/solution.py
+++ b/solution.py
@@ -189,7 +189,7 @@
     return jnp.concatenate(columns, axis=0).T[:8]
 
 
-def project(vec, res, out):
+def project(vec, res, modulus, out, to_west, to_east, to_south, to_north):
     def cell(index, totals):
         block = res[pl.ds(index, 32, stride=192), :]
         return tuple(totals[k] + block * vec[pl.ds(k * 192 + index, 1), :] for k in range(8))
@@ -197,6 +197,38 @@
     totals = lax.fori_loop(0, 192, cell, tuple(jnp.zeros((32, 128), jnp.float32) for _ in range(8)), unroll=4)
     slots = [[totals[k][8 * i : 8 * i + 8] for k in range(8)] for i in range(4)]
     out[...] = panel_of([[]] * 12 + slots)
+
+    def lines_of(index, carry):
+        for side, first in ((to_west, 0), (to_east, 48)):
+            side[pl.ds(pl.multiple_of(index * 16, 16), 16), :] = vec[pl.ds(pl.multiple_of(index * 64 + first, 16), 16), :]
+        for side, first in ((to_south, 0), (to_north, 6)):
+            for layer in range(2):
+                side[pl.ds(pl.multiple_of(index * 16 + layer * 8, 8), 8), :] = vec[
+                    pl.ds(index * 64 + first + layer, 8, stride=8), :
+                ]
+        at = pl.multiple_of(400 + index * 32, 16)
+        start = index // 8 * 64
+        place = index % 8
+        to_west[pl.ds(at, 32), :] = res[pl.ds(start + place, 32, stride=192), :]
+        to_east[pl.ds(at, 32), :] = res[pl.ds(start + 56 + place, 32, stride=192), :]
+        to_south[pl.ds(at, 32), :] = res[pl.ds(start + place * 8, 32, stride=192), :]
+        to_north[pl.ds(at, 32), :] = res[pl.ds(start + place * 8 + 7, 32, stride=192), :]
+        return carry
+
+    lax.fori_loop(0, 24, lines_of, 0, unroll=2)
+    for layer in range(2):
+        span = slice(384 + 8 * layer, 392 + 8 * layer)
+        to_west[span, :] = modulus[layer]
+        to_east[span, :] = modulus[6 + layer]
+        for side, y in ((to_south, layer), (to_north, 6 + layer)):
+            side[span, :] = jnp.concatenate([modulus[x, y : y + 1, :] for x in range(8)], axis=0)
+    for side, edge in ((to_west, 0), (to_east, 7)):
+        for start, y in ((1168, 7), (1200, 0)):
+            side[start : start + 24, :] = vec[pl.ds(edge * 8 + y, 24, stride=64), :]
+            side[start + 24 : start + 32, :] = modulus[edge]
+    blank = jnp.zeros((64, 128), jnp.float32)
+    to_south[1168:1232, :] = blank
+    to_north[1168:1232, :] = blank
 
 
 def coarse_panel(spot, vec, modulus, east, north, known, out, rows, turned):
@@ -294,15 +326,16 @@
 def coarse_rows(spot, residuals, vectors, modulus, east, north, count):
     whole = pl.BlockSpec(memory_space=pltpu.VMEM)
     vec = vectors.reshape(1536, 128)
-    known = pl.pallas_call(
+    message = jax.ShapeDtypeStruct((1232, 128), jnp.float32)
+    known, *messages = pl.pallas_call(
         project,
-        out_shape=jax.ShapeDtypeStruct((8, 128), jnp.float32),
-        in_specs=[whole, whole],
-        out_specs=whole,
+        out_shape=(jax.ShapeDtypeStruct((8, 128), jnp.float32),) + (message,) * 4,
+        in_specs=[whole] * 3,
+        out_specs=(whole,) * 5,
         compiler_params=pltpu.CompilerParams(vmem_limit_bytes=16 * 1024 * 1024),
         cost_estimate=pl.CostEstimate(flops=12_600_000, bytes_accessed=4_000_000, transcendentals=0),
-    )(vec, residuals.reshape(6144, 128))
-    return pl.pallas_call(
+    )(vec, residuals.reshape(6144, 128), modulus)
+    every = pl.pallas_call(
         coarse_panel,
         out_shape=jax.ShapeDtypeStruct((count, 8, 128), jnp.float32),
         in_specs=[pl.BlockSpec(memory_space=pltpu.SMEM)] + [whole] * 5,
@@ -311,6 +344,7 @@
         compiler_params=pltpu.CompilerParams(vmem_limit_bytes=16 * 1024 * 1024),
         cost_estimate=pl.CostEstimate(flops=6_000_000, bytes_accessed=2_000_000, transcendentals=0),
     )(spot, vec, modulus, east, north, known)
+    return every, messages
 
 
 def sweep_rows(modulus, rows):
@@ -378,23 +412,25 @@
     modulus[0:2, 2:10, :] = west[384:400, :].reshape(2, 8, 128)
     modulus[10:12, 2:10, :] = east[384:400, :].reshape(2, 8, 128)
     for x in range(8):
-        modulus[x + 2, 0:2, :] = south[384 + 2 * x : 386 + 2 * x, :]
-        modulus[x + 2, 10:12, :] = north[384 + 2 * x : 386 + 2 * x, :]
-    for y, side in ((1, south), (10, north)):
-        modulus[1, y : y + 1, :] = side[1192:1193, :]
-        modulus[10, y : y + 1, :] = side[1217:1218, :]
+        for layer in range(2):
+            row = 384 + 8 * layer + x
+            modulus[x + 2, layer : layer + 1, :] = south[row : row + 1, :]
+            modulus[x + 2, 10 + layer : 11 + layer, :] = north[row : row + 1, :]
+    for y, side, row in ((1, south, 1199), (10, north, 1192)):
+        modulus[1, y : y + 1, :] = side[row : row + 1, :]
+        modulus[10, y : y + 1, :] = side[row + 32 : row + 33, :]
     sweep_rows(modulus, rows)
 
     def edge_cells(y, carry):
         for layer in range(2):
             correct(1, layer * 12 + y + 2, west, lambda k, c: ((k * 3 + c) * 2 + layer) * 8 + y, layer == 0)
             correct(7, (10 + layer) * 12 + y + 2, east, lambda k, c: ((k * 3 + c) * 2 + layer) * 8 + y, layer == 1)
-            correct(3, (y + 2) * 12 + layer, south, lambda k, c: ((k * 3 + c) * 8 + y) * 2 + layer, layer == 0)
-            correct(5, (y + 2) * 12 + 10 + layer, north, lambda k, c: ((k * 3 + c) * 8 + y) * 2 + layer, layer == 1)
+            correct(3, (y + 2) * 12 + layer, south, lambda k, c: (k * 3 + c) * 16 + layer * 8 + y, layer == 0)
+            correct(5, (y + 2) * 12 + 10 + layer, north, lambda k, c: (k * 3 + c) * 16 + layer * 8 + y, layer == 1)
         return carry
 
     lax.fori_loop(0, 8, edge_cells, 0)
-    for x, near_x, start in ((1, 0, 1168), (10, 6, 1193)):
+    for x, near_x, start in ((1, 0, 1168), (10, 6, 1200)):
         correct(near_x, x * 12 + 1, south, lambda k, c: start + k * 3 + c, True)
         correct(near_x + 2, x * 12 + 10, north, lambda k, c: start + k * 3 + c, True)
     loads[4].wait()
@@ -403,7 +439,12 @@
         weight = rows[6, x, pl.ds(y, 1), :]
         for comp in range(3):
             scaled[x * 10 + y, comp * 32 : comp * 32 + 32, :] = (
-                source[pl.ds(start(comp), 32, stride=stride), :] * weight
+                (
+                    source[pl.ds(start(comp), 32, stride=stride), :]
+                    if stride > 1
+                    else source[pl.ds(pl.multiple_of(start(comp), 16), 32), :]
+                )
+                * weight
             )
 
     def own_scaled(index, carry):
@@ -414,10 +455,10 @@
     lax.fori_loop(0, 64, own_scaled, 0, unroll=4)
 
     def edge_scaled(y, carry):
-        scale_cell(0, y + 1, west, lambda c: 400 + c * 8 + y, 24)
-        scale_cell(9, y + 1, east, lambda c: 400 + c * 8 + y, 24)
-        scale_cell(y + 1, 0, south, lambda c: 400 + c * 8 + y, 24)
-        scale_cell(y + 1, 9, north, lambda c: 400 + c * 8 + y, 24)
+        scale_cell(0, y + 1, west, lambda c: 400 + (c * 8 + y) * 32, 1)
+        scale_cell(9, y + 1, east, lambda c: 400 + (c * 8 + y) * 32, 1)
+        scale_cell(y + 1, 0, south, lambda c: 400 + (c * 8 + y) * 32, 1)
+        scale_cell(y + 1, 9, north, lambda c: 400 + (c * 8 + y) * 32, 1)
         return carry
 
     lax.fori_loop(0, 8, edge_scaled, 0, unroll=2)
@@ -497,10 +538,10 @@
             pltpu.VMEM((100, 96, 128), jnp.float32),
             pltpu.VMEM((256, 256), jnp.bfloat16),
             pltpu.VMEM((6144, 128), jnp.float32),
-            pltpu.VMEM((1168, 128), jnp.float32),
-            pltpu.VMEM((1168, 128), jnp.float32),
-            pltpu.VMEM((1218, 128), jnp.float32),
-            pltpu.VMEM((1218, 128), jnp.float32),
+            pltpu.VMEM((1232, 128), jnp.float32),
+            pltpu.VMEM((1232, 128), jnp.float32),
+            pltpu.VMEM((1232, 128), jnp.float32),
+            pltpu.VMEM((1232, 128), jnp.float32),
             pltpu.VMEM((6144, 128), jnp.float32),
             pltpu.SemaphoreType.DMA((5,)),
             pltpu.SemaphoreType.DMA((8,)),
@@ -542,23 +583,15 @@
     east_face = shifted(lines(vectors[:, :, 0], modulus[0]), "gx", -1)
     north_face = shifted(lines(vectors[:, :, :, 0], modulus[:, 0]), "yz", -1)
     spot = jnp.stack([index_x, index_y]).astype(jnp.int32)
-    every = coarse_rows(spot, residuals, vectors, modulus, east_face, north_face, count)
-    to_west = lines(vectors[:, :, 0:2], modulus[0:2], residuals[:, :, 0])
-    to_east = lines(vectors[:, :, 6:8], modulus[6:8], residuals[:, :, 7])
-    every, to_west, to_east = lax.optimization_barrier((every, to_west, to_east))
+    every, messages = coarse_rows(spot, residuals, vectors, modulus, east_face, north_face, count)
+    every, to_west, to_east, to_south, to_north = lax.optimization_barrier((every, *messages))
     rows = lax.all_to_all(every, ("gx", "yz"), 0, 0)
     west = shifted(to_east, "gx", 1)
     east = shifted(to_west, "gx", -1)
-    south = shifted(
-        lines(vectors[:, :, :, 6:8], modulus[:, 6:8], residuals[:, :, :, 7], west[15:400:16], east[7:400:16]),
-        "yz",
-        1,
-    )
-    north = shifted(
-        lines(vectors[:, :, :, 0:2], modulus[:, 0:2], residuals[:, :, :, 0], west[8:400:16], east[0:400:16]),
-        "yz",
-        -1,
-    )
+    to_north = to_north.at[1168:1200].set(west[1168:1200]).at[1200:1232].set(east[1168:1200])
+    to_south = to_south.at[1168:1200].set(west[1200:1232]).at[1200:1232].set(east[1200:1232])
+    south = shifted(to_north, "yz", 1)
+    north = shifted(to_south, "yz", -1)
     coeffs, near = solve_rows(spot, rows, count_x, count_y * width)
     result = local_parts(near, residuals, vectors, modulus, west, east, south, north)
     return (coeffs, result)

time: 109 us -> 105 us (0.963)
  local copies, waits for them, and re-layouts: 18 us -> 8.24 us
  waiting for transfers between devices: 0.02 us -> 6.96 us
  other arithmetic: 2.86 us -> 0.97 us
  Pallas kernels: 57.9 us -> 59.1 us
    slice x9 -> x0, local copies, waits for them, and re-layouts: 8.95 us -> none  [the longest x2 2.97 us: on_device(): to_east = lines(vectors[:, :, 6:8], modulus[6:8], residuals[:, :, 7])]
    all_to_all x1, waiting for transfers between devices: 0.01 us -> 6.94 us  [on_device(): rows = lax.all_to_all(every, ('gx', 'yz'), 0, 0)]
    concatenate x2 -> x0, local copies, waits for them, and re-layouts: 3.39 us -> none  [lines(): return jnp.concatenate([array.reshape(-1, 128) for array in arrays], axis=0)]
    concatenate x3 -> x2, other arithmetic: 1.77 us -> 0.02 us  [lines(): return jnp.concatenate([array.reshape(-1, 128) for array in arrays], axis=0)]
    scatter x0 -> x2, local copies, waits for them, and re-layouts: none -> 1.48 us  [on_device(): to_south.at[1168:1200].set(west[1200:1232]).at[1200:1232]]
    pallas_call x1, Pallas kernels: 4.22 us -> 5.4 us  [coarse_rows(): pl.pallas_call(project, out_shape=(jax.ShapeDtypeStruct((8, 128), jnp.flo...]
    unnamed x20 -> x12, local copies, waits for them, and re-layouts: 3.58 us -> 4.67 us
  transfers between devices with their start and end apart: 7 -> 7, of which waited for: 0 -> 1; matrix products, arithmetic and copies ran while one was open for 14% -> 3% of each run, Pallas kernels for 27% -> 28%
where the time goes in v4:
time: 105 us
  Pallas kernels  59.1 us (56%)
  starting transfers between devices  28.4 us (27%)
  local copies, waits for them, and re-layouts  8.24 us (8%)
  waiting for transfers between devices  6.96 us (7%)
    pallas_call x1, Pallas kernels, solve_rows(): pl.pallas_call(functools.partial(coarse_solve, slabs, size, chunk), out_s...  24.1 us
    pallas_call x1, Pallas kernels, local_parts(): pl.pallas_call(local_stage, out_shape=jax.ShapeDtypeStruct((96, 8, 8, 128...  23.1 us
    ppermute x6, starting transfers between devices, shifted(): lax.ppermute(values, axis, [(i, i + step) for i in range(count) if 0 <= i...  15.1 us
    all_to_all x1, starting transfers between devices, on_device(): rows = lax.all_to_all(every, ('gx', 'yz'), 0, 0)  13.4 us
    all_to_all x1, waiting for transfers between devices, on_device(): rows = lax.all_to_all(every, ('gx', 'yz'), 0, 0)  6.94 us
    pallas_call x1, Pallas kernels, coarse_rows(): pl.pallas_call(coarse_panel, out_shape=jax.ShapeDtypeStruct((count, 8, 12...  6.47 us
    pallas_call x1, Pallas kernels, coarse_rows(): pl.pallas_call(project, out_shape=(jax.ShapeDtypeStruct((8, 128), jnp.flo...  5.4 us
    unnamed x12, local copies, waits for them, and re-layouts  4.67 us
  transfers between devices with their start and end apart: 7, of which 1 were waited for; matrix products, arithmetic and copies ran while one was open for 3% of the time, Pallas kernels for 28%

profile of v4, /device:TPU:1, one launch (start us, length us, event | category | flops | bytes accessed | tf_op | source)
XLA Modules:
  0.0 104.5 jit_solution(1675732919010790943)
XLA Ops:
  0.6 0.9 select_reduce_fusion.modulus.own_mod
  1.5 0.0 copy-start.2
  1.5 0.9 slice.92
  2.4 3.3 %collective-permute-start = (f32[200,128]{1,0:T(8,128)S(1)}, f32[200,128]{1,0:T(8,128)S(1)}, u32[]{:S(2)}, u32[]{:S(2)}) collective-permute-start(f32[200,128]{1,0:T(8,128)S(1)} %pad_maximum_fusion), channel_id=1, source_target_pairs={{4,0},{8,4},{12,8},{16,12},{20,16},{24,20},{28,24},{32,28},{36,32}... | collective-permute-start | bytes 307208 | tf_op jit(solution)/shard_map/ppermute | solution.py:564
  5.8 1.2 %slice.94 = f32[8,3,8,1,128]{4,3,2,1,0:T(1,128)S(1)} slice(f32[8,3,8,8,128]{4,3,2,1,0:T(8,128)} %param.13), slice={[0:8], [0:3], [0:8], [0:1], [0:128]} | slice | bytes 196608 | tf_op jit(solution)/shard_map/slice | solution.py:584
  7.0 1.3 %collective-permute-start.1 = (f32[200,128]{1,0:T(8,128)S(1)}, f32[200,128]{1,0:T(8,128)S(1)}, u32[]{:S(2)}, u32[]{:S(2)}) collective-permute-start(f32[200,128]{1,0:T(8,128)S(1)} %pad_maximum_fusion.1), channel_id=1, source_target_pairs={{1,0},{2,1},{3,2},{5,4},{6,5},{7,6},{9,8},{10,9},{11,10},{13,12},{... | collective-permute-start | bytes 307208 | tf_op jit(solution)/shard_map/ppermute | solution.py:564
  8.3 0.0 copy-start
  8.3 1.9 %copy-done = f32[32,3,8,8,128]{4,3,2,1,0:T(8,128)S(1)} copy-done((f32[32,3,8,8,128]{4,3,2,1,0:T(8,128)S(1)}, f32[32,3,8,8,128]{4,3,2,1,0:T(8,128)}, u32[]{:S(2)}) %copy-start) | copy-done | bytes 3145752
  10.2 1.1 %copy-done.1 = f32[8,3,8,8,128]{4,3,2,1,0:T(8,128)S(1)} copy-done((f32[8,3,8,8,128]{4,3,2,1,0:T(8,128)S(1)}, f32[8,3,8,8,128]{4,3,2,1,0:T(8,128)}, u32[]{:S(2)}) %copy-start.1) | copy-done | bytes 786456
  11.3 5.4 %shard_map.59 = (f32[8,128]{1,0:T(8,128)S(1)}, f32[1232,128]{1,0:T(8,128)S(1)}, f32[1232,128]{1,0:T(8,128)S(1)}, f32[1232,128]{1,0:T(8,128)S(1)}, f32[1232,128]{1,0:T(8,128)S(1)}) custom-call(f32[1536,128]{1,0:T(8,128)S(1)} %bitcast.15, f32[6144,128]{1,0:T(8,128)S(1)} %bitcast.13, f32[8,8,128]{2,1,0:T(8,128)S(1)} %select_reduce_fusion.modulus.own_mod), custom_call_target="tpu_custom_call" | custom-call | flops 12600000 | bytes 4000000 | tf_op jit(solution)/shard_map/pallas_call | solution.py:330
  16.7 0.1 pad_add_fusion.spot
  16.8 0.0 collective-permute-done.east
  16.8 0.0 collective-permute-done.1.north
  16.8 6.5 %shard_map.60 = f32[128,8,128]{2,1,0:T(8,128)} custom-call(s32[2]{0:T(128)S(1)} %pad_add_fusion.spot, f32[1536,128]{1,0:T(8,128)S(1)} %bitcast.16, f32[8,8,128]{2,1,0:T(8,128)S(1)} %select_reduce_fusion.modulus.own_mod, f32[200,128]{1,0:T(8,128)S(1)} %collective-permute-done.east, f32[200,128]{1,0:T(8,128)S(1)} %collective-permute-done.1.north, ...), custom_call_target="tpu_custom_call" | custom-call | flops 6000000 | bytes 2000000 | tf_op jit(solution)/shard_map/pallas_call | solution.py:338
  23.3 0.0 copy-done.2
  23.3 3.1 %collective-permute-start.2 = (f32[1232,128]{1,0:T(8,128)S(1)}, f32[1232,128]{1,0:T(8,128)}, u32[]{:S(2)}, u32[]{:S(2)}) collective-permute-start(f32[1232,128]{1,0:T(8,128)S(1)} %get-tuple-element.70), channel_id=1, source_target_pairs={{0,4},{4,8},{8,12},{12,16},{16,20},{20,24},{24,28},{28,32},{32,36}... | collective-permute-start | bytes 1892360 | tf_op jit(solution)/shard_map/ppermute | solution.py:564
  26.4 2.1 %collective-permute-start.3 = (f32[1232,128]{1,0:T(8,128)S(1)}, f32[1232,128]{1,0:T(8,128)}, u32[]{:S(2)}, u32[]{:S(2)}) collective-permute-start(f32[1232,128]{1,0:T(8,128)S(1)} %get-tuple-element.71), channel_id=1, source_target_pairs={{4,0},{8,4},{12,8},{16,12},{20,16},{24,20},{28,24},{32,28},{36,32}... | collective-permute-start | bytes 1892360 | tf_op jit(solution)/shard_map/ppermute | solution.py:564
  28.5 13.4 %all-to-all-start = ((f32[128,8,128]{2,1,0:T(8,128)}), f32[128,8,128]{2,1,0:T(8,128)S(1)}, u32[]{:S(2)}, u32[]{:S(2)}) async-start(f32[128,8,128]{2,1,0:T(8,128)} %shard_map.60), calls=%async_computation | async-start | bytes 1048576 | tf_op jit(solution)/shard_map/all_to_all | solution.py:588
  41.8 0.0 collective-permute-done.2.west_far
  41.8 0.7 slice_dynamic-update-slice_fusion.1
  42.6 0.0 collective-permute-done.3.east_far
  42.6 0.7 slice_dynamic-update-slice_fusion
  43.3 1.3 %collective-permute-start.5 = (f32[1232,128]{1,0:T(8,128)S(1)}, f32[1232,128]{1,0:T(8,128)S(1)}, u32[]{:S(2)}, u32[]{:S(2)}) collective-permute-start(f32[1232,128]{1,0:T(8,128)S(1)} %get-tuple-element.74), channel_id=1, source_target_pairs={{1,0},{2,1},{3,2},{5,4},{6,5},{7,6},{9,8},{10,9},{11,10},{13,12},{... | collective-permute-start | bytes 1892360 | tf_op jit(solution)/shard_map/ppermute | solution.py:564
  44.6 4.0 %collective-permute-start.4 = (f32[1232,128]{1,0:T(8,128)S(1)}, f32[1232,128]{1,0:T(8,128)S(1)}, u32[]{:S(2)}, u32[]{:S(2)}) collective-permute-start(f32[1232,128]{1,0:T(8,128)S(1)} %get-tuple-element.75), channel_id=1, source_target_pairs={{0,1},{1,2},{2,3},{4,5},{5,6},{6,7},{8,9},{9,10},{10,11},{12,13},{... | collective-permute-start | bytes 1892360 | tf_op jit(solution)/shard_map/ppermute | solution.py:564
  48.6 6.9 %all-to-all-done.rows_ref = f32[128,8,128]{2,1,0:T(8,128)S(1)} async-done(((f32[128,8,128]{2,1,0:T(8,128)}), f32[128,8,128]{2,1,0:T(8,128)S(1)}, u32[]{:S(2)}, u32[]{:S(2)}) %all-to-all-start) | async-done | bytes 524320 | tf_op jit(solution)/shard_map/all_to_all | solution.py:588
  55.6 24.1 %shard_map.61 = (f32[8,32]{1,0:T(8,128)}, f32[72,32]{1,0:T(8,128)S(1)}) custom-call(s32[2]{0:T(128)S(1)} %pad_add_fusion.spot, f32[128,8,128]{2,1,0:T(8,128)S(1)} %all-to-all-done.rows_ref), custom_call_target="tpu_custom_call" | custom-call | flops 20000000000 | bytes 90000000 | tf_op jit(solution)/shard_map/pallas_call | solution.py:159
  79.7 0.6 copy-done.3
  80.3 0.0 collective-permute-done.5.north_far
  80.3 0.0 collective-permute-done.4.south_far
  80.4 0.8 copy-done.4
  81.2 0.2 copy-done.5
  81.4 23.1 %shard_map.62 = f32[96,8,8,128]{3,2,1,0:T(8,128)} custom-call(f32[72,32]{1,0:T(8,128)} %copy-done.3, f32[6144,128]{1,0:T(8,128)} %bitcast.12, f32[1536,128]{1,0:T(8,128)} %bitcast.14, f32[8,8,128]{2,1,0:T(8,128)} %copy-done.2, f32[1232,128]{1,0:T(8,128)} %collective-permute-done.2.west_far, f32[1232,128]{1,0:T(8,128)} %collective-permute-done.3.east_far, ...), custom_call_target="tpu_custom_call" | custom-call | tf_op jit(solution)/shard_map/pallas_call | solution.py:527
  (8 shorter events, 0.0 us)
Async XLA Ops:
  1.5 21.8 %copy-start.2 = (f32[8,8,128]{2,1,0:T(8,128)}, f32[8,8,128]{2,1,0:T(8,128)S(1)}, u32[]{:S(2)}) copy-start(f32[8,8,128]{2,1,0:T(8,128)S(1)} %select_reduce_fusion.modulus.own_mod) | copy-start | bytes 98308
  2.4 14.4 %collective-permute-start = (f32[200,128]{1,0:T(8,128)S(1)}, f32[200,128]{1,0:T(8,128)S(1)}, u32[]{:S(2)}, u32[]{:S(2)}) collective-permute-start(f32[200,128]{1,0:T(8,128)S(1)} %pad_maximum_fusion), channel_id=1, source_target_pairs={{4,0},{8,4},{12,8},{16,12},{20,16},{24,20},{28,24},{32,28},{36,32}... | collective-permute-start | bytes 307208 | tf_op jit(solution)/shard_map/ppermute | solution.py:564
  7.0 9.8 %collective-permute-start.1 = (f32[200,128]{1,0:T(8,128)S(1)}, f32[200,128]{1,0:T(8,128)S(1)}, u32[]{:S(2)}, u32[]{:S(2)}) collective-permute-start(f32[200,128]{1,0:T(8,128)S(1)} %pad_maximum_fusion.1), channel_id=1, source_target_pairs={{1,0},{2,1},{3,2},{5,4},{6,5},{7,6},{9,8},{10,9},{11,10},{13,12},{... | collective-permute-start | bytes 307208 | tf_op jit(solution)/shard_map/ppermute | solution.py:564
  8.3 1.9 %copy-start = (f32[32,3,8,8,128]{4,3,2,1,0:T(8,128)S(1)}, f32[32,3,8,8,128]{4,3,2,1,0:T(8,128)}, u32[]{:S(2)}) copy-start(f32[32,3,8,8,128]{4,3,2,1,0:T(8,128)} %param.12) | copy-start | bytes 9437188
  10.2 1.1 %copy-start.1 = (f32[8,3,8,8,128]{4,3,2,1,0:T(8,128)S(1)}, f32[8,3,8,8,128]{4,3,2,1,0:T(8,128)}, u32[]{:S(2)}) copy-start(f32[8,3,8,8,128]{4,3,2,1,0:T(8,128)} %param.13) | copy-start | bytes 2359300
  23.3 18.5 %collective-permute-start.2 = (f32[1232,128]{1,0:T(8,128)S(1)}, f32[1232,128]{1,0:T(8,128)}, u32[]{:S(2)}, u32[]{:S(2)}) collective-permute-start(f32[1232,128]{1,0:T(8,128)S(1)} %get-tuple-element.70), channel_id=1, source_target_pairs={{0,4},{4,8},{8,12},{12,16},{16,20},{20,24},{24,28},{28,32},{32,36}... | collective-permute-start | bytes 1892360 | tf_op jit(solution)/shard_map/ppermute | solution.py:564
  26.4 16.2 %collective-permute-start.3 = (f32[1232,128]{1,0:T(8,128)S(1)}, f32[1232,128]{1,0:T(8,128)}, u32[]{:S(2)}, u32[]{:S(2)}) collective-permute-start(f32[1232,128]{1,0:T(8,128)S(1)} %get-tuple-element.71), channel_id=1, source_target_pairs={{4,0},{8,4},{12,8},{16,12},{20,16},{24,20},{28,24},{32,28},{36,32}... | collective-permute-start | bytes 1892360 | tf_op jit(solution)/shard_map/ppermute | solution.py:564
  28.5 27.1 %all-to-all-start = ((f32[128,8,128]{2,1,0:T(8,128)}), f32[128,8,128]{2,1,0:T(8,128)S(1)}, u32[]{:S(2)}, u32[]{:S(2)}) async-start(f32[128,8,128]{2,1,0:T(8,128)} %shard_map.60), calls=%async_computation | async-start | bytes 1048576 | tf_op jit(solution)/shard_map/all_to_all | solution.py:588
  43.3 37.0 %collective-permute-start.5 = (f32[1232,128]{1,0:T(8,128)S(1)}, f32[1232,128]{1,0:T(8,128)S(1)}, u32[]{:S(2)}, u32[]{:S(2)}) collective-permute-start(f32[1232,128]{1,0:T(8,128)S(1)} %get-tuple-element.74), channel_id=1, source_target_pairs={{1,0},{2,1},{3,2},{5,4},{6,5},{7,6},{9,8},{10,9},{11,10},{13,12},{... | collective-permute-start | bytes 1892360 | tf_op jit(solution)/shard_map/ppermute | solution.py:564
  44.6 35.7 %collective-permute-start.4 = (f32[1232,128]{1,0:T(8,128)S(1)}, f32[1232,128]{1,0:T(8,128)S(1)}, u32[]{:S(2)}, u32[]{:S(2)}) collective-permute-start(f32[1232,128]{1,0:T(8,128)S(1)} %get-tuple-element.75), channel_id=1, source_target_pairs={{0,1},{1,2},{2,3},{4,5},{5,6},{6,7},{8,9},{9,10},{10,11},{12,13},{... | collective-permute-start | bytes 1892360 | tf_op jit(solution)/shard_map/ppermute | solution.py:564
  79.7 0.6 copy-start.3
  80.3 0.8 copy-start.4
  80.4 1.0 copy-start.5

commit v5 on v4

--- a/solution.py
+++ b/solution.py
@@ -91,7 +91,7 @@
         slab(g, False)
         return carry
 
-    lax.fori_loop(1, slabs, later, 0)
+    lax.fori_loop(1, slabs, later, 0, unroll=4)
 
 
 def coarse_solve(slabs, size, chunk, spot, rows_ref, own_ref, near_ref, work, found):
@@ -301,7 +301,7 @@
                 ]
             return tuple(new)
 
-        return lax.fori_loop(0, 24, spot_of, (zero,) * 24)
+        return lax.fori_loop(0, 24, spot_of, (zero,) * 24, unroll=4)
 
     easts = face(east, 56, 1, 7)
     norths = face(north, 7, 8, 8)
@@ -429,7 +429,7 @@
             correct(5, (y + 2) * 12 + 10 + layer, north, lambda k, c: (k * 3 + c) * 16 + layer * 8 + y, layer == 1)
         return carry
 
-    lax.fori_loop(0, 8, edge_cells, 0)
+    lax.fori_loop(0, 8, edge_cells, 0, unroll=2)
     for x, near_x, start in ((1, 0, 1168), (10, 6, 1200)):
         correct(near_x, x * 12 + 1, south, lambda k, c: start + k * 3 + c, True)
         correct(near_x + 2, x * 12 + 10, north, lambda k, c: start + k * 3 + c, True)

time: 105 us -> 103 us (0.981)
  Pallas kernels: 59.1 us -> 57.2 us
    pallas_call x1, Pallas kernels: 24.1 us -> 22.7 us  [solve_rows(): pl.pallas_call(functools.partial(coarse_solve, slabs, size, chunk), out_s...]
  transfers between devices with their start and end apart: 7 -> 7, of which waited for: 1 -> 1; matrix products, arithmetic and copies ran while one was open for 3% -> 3% of each run, Pallas kernels for 28% -> 27%
where the time goes in v5:
time: 103 us
  Pallas kernels  57.2 us (56%)
  starting transfers between devices  28.6 us (28%)
  local copies, waits for them, and re-layouts  8.24 us (8%)
  waiting for transfers between devices  6.78 us (7%)
    pallas_call x1, Pallas kernels, local_parts(): pl.pallas_call(local_stage, out_shape=jax.ShapeDtypeStruct((96, 8, 8, 128...  23.1 us
    pallas_call x1, Pallas kernels, solve_rows(): pl.pallas_call(functools.partial(coarse_solve, slabs, size, chunk), out_s...  22.7 us
    ppermute x6, starting transfers between devices, shifted(): lax.ppermute(values, axis, [(i, i + step) for i in range(count) if 0 <= i...  15.3 us
    all_to_all x1, starting transfers between devices, on_device(): rows = lax.all_to_all(every, ('gx', 'yz'), 0, 0)  13.4 us
    all_to_all x1, waiting for transfers between devices, on_device(): rows = lax.all_to_all(every, ('gx', 'yz'), 0, 0)  6.76 us
    pallas_call x1, Pallas kernels, coarse_rows(): pl.pallas_call(coarse_panel, out_shape=jax.ShapeDtypeStruct((count, 8, 12...  5.97 us
    pallas_call x1, Pallas kernels, coarse_rows(): pl.pallas_call(project, out_shape=(jax.ShapeDtypeStruct((8, 128), jnp.flo...  5.4 us
    unnamed x12, local copies, waits for them, and re-layouts  4.67 us
  transfers between devices with their start and end apart: 7, of which 1 were waited for; matrix products, arithmetic and copies ran while one was open for 3% of the time, Pallas kernels for 27%

profile of v5, /device:TPU:1, one launch (start us, length us, event | category | flops | bytes accessed | tf_op | source)
XLA Modules:
  0.0 102.7 jit_solution(12017277063034928038)
XLA Ops:
  0.6 0.9 select_reduce_fusion.modulus.own_mod
  1.5 0.0 copy-start.2
  1.5 0.9 slice.92
  2.4 3.3 %collective-permute-start = (f32[200,128]{1,0:T(8,128)S(1)}, f32[200,128]{1,0:T(8,128)S(1)}, u32[]{:S(2)}, u32[]{:S(2)}) collective-permute-start(f32[200,128]{1,0:T(8,128)S(1)} %pad_maximum_fusion), channel_id=1, source_target_pairs={{4,0},{8,4},{12,8},{16,12},{20,16},{24,20},{28,24},{32,28},{36,32}... | collective-permute-start | bytes 307208 | tf_op jit(solution)/shard_map/ppermute | solution.py:564
  5.8 1.2 %slice.94 = f32[8,3,8,1,128]{4,3,2,1,0:T(1,128)S(1)} slice(f32[8,3,8,8,128]{4,3,2,1,0:T(8,128)} %param.13), slice={[0:8], [0:3], [0:8], [0:1], [0:128]} | slice | bytes 196608 | tf_op jit(solution)/shard_map/slice | solution.py:584
  7.0 1.3 %collective-permute-start.1 = (f32[200,128]{1,0:T(8,128)S(1)}, f32[200,128]{1,0:T(8,128)S(1)}, u32[]{:S(2)}, u32[]{:S(2)}) collective-permute-start(f32[200,128]{1,0:T(8,128)S(1)} %pad_maximum_fusion.1), channel_id=1, source_target_pairs={{1,0},{2,1},{3,2},{5,4},{6,5},{7,6},{9,8},{10,9},{11,10},{13,12},{... | collective-permute-start | bytes 307208 | tf_op jit(solution)/shard_map/ppermute | solution.py:564
  8.3 0.0 copy-start
  8.3 1.9 %copy-done = f32[32,3,8,8,128]{4,3,2,1,0:T(8,128)S(1)} copy-done((f32[32,3,8,8,128]{4,3,2,1,0:T(8,128)S(1)}, f32[32,3,8,8,128]{4,3,2,1,0:T(8,128)}, u32[]{:S(2)}) %copy-start) | copy-done | bytes 3145752
  10.2 1.1 %copy-done.1 = f32[8,3,8,8,128]{4,3,2,1,0:T(8,128)S(1)} copy-done((f32[8,3,8,8,128]{4,3,2,1,0:T(8,128)S(1)}, f32[8,3,8,8,128]{4,3,2,1,0:T(8,128)}, u32[]{:S(2)}) %copy-start.1) | copy-done | bytes 786456
  11.3 5.4 %shard_map.59 = (f32[8,128]{1,0:T(8,128)S(1)}, f32[1232,128]{1,0:T(8,128)S(1)}, f32[1232,128]{1,0:T(8,128)S(1)}, f32[1232,128]{1,0:T(8,128)S(1)}, f32[1232,128]{1,0:T(8,128)S(1)}) custom-call(f32[1536,128]{1,0:T(8,128)S(1)} %bitcast.15, f32[6144,128]{1,0:T(8,128)S(1)} %bitcast.13, f32[8,8,128]{2,1,0:T(8,128)S(1)} %select_reduce_fusion.modulus.own_mod), custom_call_target="tpu_custom_call" | custom-call | flops 12600000 | bytes 4000000 | tf_op jit(solution)/shard_map/pallas_call | solution.py:330
  16.7 0.1 pad_add_fusion.spot
  16.8 0.0 collective-permute-done.east
  16.8 0.0 collective-permute-done.1.north
  16.8 6.0 %shard_map.60 = f32[128,8,128]{2,1,0:T(8,128)} custom-call(s32[2]{0:T(128)S(1)} %pad_add_fusion.spot, f32[1536,128]{1,0:T(8,128)S(1)} %bitcast.16, f32[8,8,128]{2,1,0:T(8,128)S(1)} %select_reduce_fusion.modulus.own_mod, f32[200,128]{1,0:T(8,128)S(1)} %collective-permute-done.east, f32[200,128]{1,0:T(8,128)S(1)} %collective-permute-done.1.north, ...), custom_call_target="tpu_custom_call" | custom-call | flops 6000000 | bytes 2000000 | tf_op jit(solution)/shard_map/pallas_call | solution.py:338
  22.8 3.1 %collective-permute-start.2 = (f32[1232,128]{1,0:T(8,128)S(1)}, f32[1232,128]{1,0:T(8,128)}, u32[]{:S(2)}, u32[]{:S(2)}) collective-permute-start(f32[1232,128]{1,0:T(8,128)S(1)} %get-tuple-element.70), channel_id=1, source_target_pairs={{0,4},{4,8},{8,12},{12,16},{16,20},{20,24},{24,28},{28,32},{32,36}... | collective-permute-start | bytes 1892360 | tf_op jit(solution)/shard_map/ppermute | solution.py:564
  25.9 2.1 %collective-permute-start.3 = (f32[1232,128]{1,0:T(8,128)S(1)}, f32[1232,128]{1,0:T(8,128)}, u32[]{:S(2)}, u32[]{:S(2)}) collective-permute-start(f32[1232,128]{1,0:T(8,128)S(1)} %get-tuple-element.71), channel_id=1, source_target_pairs={{4,0},{8,4},{12,8},{16,12},{20,16},{24,20},{28,24},{32,28},{36,32}... | collective-permute-start | bytes 1892360 | tf_op jit(solution)/shard_map/ppermute | solution.py:564
  28.0 13.4 %all-to-all-start = ((f32[128,8,128]{2,1,0:T(8,128)}), f32[128,8,128]{2,1,0:T(8,128)S(1)}, u32[]{:S(2)}, u32[]{:S(2)}) async-start(f32[128,8,128]{2,1,0:T(8,128)} %shard_map.60), calls=%async_computation | async-start | bytes 1048576 | tf_op jit(solution)/shard_map/all_to_all | solution.py:588
  41.3 0.0 collective-permute-done.2.west_far
  41.3 0.7 slice_dynamic-update-slice_fusion.1
  42.1 0.0 collective-permute-done.3.east_far
  42.1 0.7 slice_dynamic-update-slice_fusion
  42.8 1.3 %collective-permute-start.5 = (f32[1232,128]{1,0:T(8,128)S(1)}, f32[1232,128]{1,0:T(8,128)S(1)}, u32[]{:S(2)}, u32[]{:S(2)}) collective-permute-start(f32[1232,128]{1,0:T(8,128)S(1)} %get-tuple-element.74), channel_id=1, source_target_pairs={{1,0},{2,1},{3,2},{5,4},{6,5},{7,6},{9,8},{10,9},{11,10},{13,12},{... | collective-permute-start | bytes 1892360 | tf_op jit(solution)/shard_map/ppermute | solution.py:564
  44.1 4.2 %collective-permute-start.4 = (f32[1232,128]{1,0:T(8,128)S(1)}, f32[1232,128]{1,0:T(8,128)S(1)}, u32[]{:S(2)}, u32[]{:S(2)}) collective-permute-start(f32[1232,128]{1,0:T(8,128)S(1)} %get-tuple-element.75), channel_id=1, source_target_pairs={{0,1},{1,2},{2,3},{4,5},{5,6},{6,7},{8,9},{9,10},{10,11},{12,13},{... | collective-permute-start | bytes 1892360 | tf_op jit(solution)/shard_map/ppermute | solution.py:564
  48.3 6.8 %all-to-all-done.rows_ref = f32[128,8,128]{2,1,0:T(8,128)S(1)} async-done(((f32[128,8,128]{2,1,0:T(8,128)}), f32[128,8,128]{2,1,0:T(8,128)S(1)}, u32[]{:S(2)}, u32[]{:S(2)}) %all-to-all-start) | async-done | bytes 524320 | tf_op jit(solution)/shard_map/all_to_all | solution.py:588
  55.1 22.7 %shard_map.61 = (f32[8,32]{1,0:T(8,128)}, f32[72,32]{1,0:T(8,128)S(1)}) custom-call(s32[2]{0:T(128)S(1)} %pad_add_fusion.spot, f32[128,8,128]{2,1,0:T(8,128)S(1)} %all-to-all-done.rows_ref), custom_call_target="tpu_custom_call" | custom-call | flops 20000000000 | bytes 90000000 | tf_op jit(solution)/shard_map/pallas_call | solution.py:159
  77.8 0.6 copy-done.3
  78.4 0.0 collective-permute-done.5.north_far
  78.4 0.0 collective-permute-done.4.south_far
  78.4 0.0 copy-start.5
  78.4 0.8 copy-done.4
  79.2 0.2 copy-done.5
  79.4 23.1 %shard_map.62 = f32[96,8,8,128]{3,2,1,0:T(8,128)} custom-call(f32[72,32]{1,0:T(8,128)} %copy-done.3, f32[6144,128]{1,0:T(8,128)} %bitcast.12, f32[1536,128]{1,0:T(8,128)} %bitcast.14, f32[8,8,128]{2,1,0:T(8,128)} %copy-done.2, f32[1232,128]{1,0:T(8,128)} %collective-permute-done.2.west_far, f32[1232,128]{1,0:T(8,128)} %collective-permute-done.3.east_far, ...), custom_call_target="tpu_custom_call" | custom-call | tf_op jit(solution)/shard_map/pallas_call | solution.py:527
  (8 shorter events, 0.0 us)
Async XLA Ops:
  1.5 21.3 %copy-start.2 = (f32[8,8,128]{2,1,0:T(8,128)}, f32[8,8,128]{2,1,0:T(8,128)S(1)}, u32[]{:S(2)}) copy-start(f32[8,8,128]{2,1,0:T(8,128)S(1)} %select_reduce_fusion.modulus.own_mod) | copy-start | bytes 98308
  2.4 14.4 %collective-permute-start = (f32[200,128]{1,0:T(8,128)S(1)}, f32[200,128]{1,0:T(8,128)S(1)}, u32[]{:S(2)}, u32[]{:S(2)}) collective-permute-start(f32[200,128]{1,0:T(8,128)S(1)} %pad_maximum_fusion), channel_id=1, source_target_pairs={{4,0},{8,4},{12,8},{16,12},{20,16},{24,20},{28,24},{32,28},{36,32}... | collective-permute-start | bytes 307208 | tf_op jit(solution)/shard_map/ppermute | solution.py:564
  7.0 9.8 %collective-permute-start.1 = (f32[200,128]{1,0:T(8,128)S(1)}, f32[200,128]{1,0:T(8,128)S(1)}, u32[]{:S(2)}, u32[]{:S(2)}) collective-permute-start(f32[200,128]{1,0:T(8,128)S(1)} %pad_maximum_fusion.1), channel_id=1, source_target_pairs={{1,0},{2,1},{3,2},{5,4},{6,5},{7,6},{9,8},{10,9},{11,10},{13,12},{... | collective-permute-start | bytes 307208 | tf_op jit(solution)/shard_map/ppermute | solution.py:564
  8.3 1.9 %copy-start = (f32[32,3,8,8,128]{4,3,2,1,0:T(8,128)S(1)}, f32[32,3,8,8,128]{4,3,2,1,0:T(8,128)}, u32[]{:S(2)}) copy-start(f32[32,3,8,8,128]{4,3,2,1,0:T(8,128)} %param.12) | copy-start | bytes 9437188
  10.2 1.1 %copy-start.1 = (f32[8,3,8,8,128]{4,3,2,1,0:T(8,128)S(1)}, f32[8,3,8,8,128]{4,3,2,1,0:T(8,128)}, u32[]{:S(2)}) copy-start(f32[8,3,8,8,128]{4,3,2,1,0:T(8,128)} %param.13) | copy-start | bytes 2359300
  22.8 18.5 %collective-permute-start.2 = (f32[1232,128]{1,0:T(8,128)S(1)}, f32[1232,128]{1,0:T(8,128)}, u32[]{:S(2)}, u32[]{:S(2)}) collective-permute-start(f32[1232,128]{1,0:T(8,128)S(1)} %get-tuple-element.70), channel_id=1, source_target_pairs={{0,4},{4,8},{8,12},{12,16},{16,20},{20,24},{24,28},{28,32},{32,36}... | collective-permute-start | bytes 1892360 | tf_op jit(solution)/shard_map/ppermute | solution.py:564
  25.9 16.2 %collective-permute-start.3 = (f32[1232,128]{1,0:T(8,128)S(1)}, f32[1232,128]{1,0:T(8,128)}, u32[]{:S(2)}, u32[]{:S(2)}) collective-permute-start(f32[1232,128]{1,0:T(8,128)S(1)} %get-tuple-element.71), channel_id=1, source_target_pairs={{4,0},{8,4},{12,8},{16,12},{20,16},{24,20},{28,24},{32,28},{36,32}... | collective-permute-start | bytes 1892360 | tf_op jit(solution)/shard_map/ppermute | solution.py:564
  28.0 27.1 %all-to-all-start = ((f32[128,8,128]{2,1,0:T(8,128)}), f32[128,8,128]{2,1,0:T(8,128)S(1)}, u32[]{:S(2)}, u32[]{:S(2)}) async-start(f32[128,8,128]{2,1,0:T(8,128)} %shard_map.60), calls=%async_computation | async-start | bytes 1048576 | tf_op jit(solution)/shard_map/all_to_all | solution.py:588
  42.8 35.6 %collective-permute-start.5 = (f32[1232,128]{1,0:T(8,128)S(1)}, f32[1232,128]{1,0:T(8,128)S(1)}, u32[]{:S(2)}, u32[]{:S(2)}) collective-permute-start(f32[1232,128]{1,0:T(8,128)S(1)} %get-tuple-element.74), channel_id=1, source_target_pairs={{1,0},{2,1},{3,2},{5,4},{6,5},{7,6},{9,8},{10,9},{11,10},{13,12},{... | collective-permute-start | bytes 1892360 | tf_op jit(solution)/shard_map/ppermute | solution.py:564
  44.1 34.3 %collective-permute-start.4 = (f32[1232,128]{1,0:T(8,128)S(1)}, f32[1232,128]{1,0:T(8,128)S(1)}, u32[]{:S(2)}, u32[]{:S(2)}) collective-permute-start(f32[1232,128]{1,0:T(8,128)S(1)} %get-tuple-element.75), channel_id=1, source_target_pairs={{0,1},{1,2},{2,3},{4,5},{5,6},{6,7},{8,9},{9,10},{10,11},{12,13},{... | collective-permute-start | bytes 1892360 | tf_op jit(solution)/shard_map/ppermute | solution.py:564
  77.8 0.6 copy-start.3
  78.4 0.8 copy-start.4
  78.4 1.0 %copy-start.5 = (f32[1232,128]{1,0:T(8,128)}, f32[1232,128]{1,0:T(8,128)S(1)}, u32[]{:S(2)}) copy-start(f32[1232,128]{1,0:T(8,128)S(1)} %collective-permute-done.4.south_far) | copy-start | bytes 1892356
